TPU v7x, 32 devices: a whole 2x2x4 slice. The times are simulated.
32 devices in a mesh: scene: 4 (over y, x), tile: 8 (over z, core).
Axes of the slice: x: 2, y: 2, z: 4, core: 2. Of those that a mesh axis runs over, the one named last changes fastest.
Arguments:
- level0: bfloat16 [4, 8, 32, 32, 256], P('scene', 'tile'), may hold values from -6 to 6
- level1: bfloat16 [4, 8, 16, 16, 256], P('scene', 'tile'), may hold values from -6 to 6
- conv_weight: bfloat16 [3, 3, 256, 256], replicated, may hold values from -0.125 to 0.125
- deconv_weight: bfloat16 [2, 2, 256, 256], replicated, may hold values from -0.375 to 0.375
- mask_weight: bfloat16 [80, 256], replicated, may hold values from -0.375 to 0.375
- crop_level: int32 [4, 8, 24], P('scene', 'tile'), may hold values from 0 to 1
- crop_row: int32 [4, 8, 24], P('scene', 'tile'), may hold values from 0 to 18, as said below
- crop_col: int32 [4, 8, 24], P('scene', 'tile'), may hold values from 0 to 18, as said below
- roi_slot: int32 [4, 8, 22], P('scene', 'tile'), may hold values from 0 to 23, as said below
- roi_class: int32 [4, 8, 22], P('scene', 'tile'), may hold values from 0 to 79
- mask_target: int32 [4, 8, 22, 28, 28], P('scene', 'tile'), may hold values 0 or 1
Outputs:
- grad_level0: float32 [4, 8, 32, 32, 256], P('scene', 'tile')
- grad_level1: float32 [4, 8, 16, 16, 256], P('scene', 'tile')
- grad_mask: float32 [80, 256], P(None, 'tile')
- roi_loss: float32 [4, 8, 22], P('scene', 'tile')
Inputs may be any that keep to these rules, and one draw needn't show every extreme that they name: `roi_slot`: each entry is tile * 3 + k with k < 3; the 22 entries of one head owner are distinct; a head owner takes at most 3 RoIs from one tile, and some head owner takes exactly 3 from some tile. A crop lies inside the tile of its level: crop_row + 14 is at most 32 for level 0 and 16 for level 1. A crop lies inside the tile of its level: crop_col + 14 is at most 32 for level 0 and 16 for level 1.
All inputs are finite; a program needn't handle non-finite values. No bound on the sum of `mask_target` on one device may be relied on, other than what follows from the above.
Results may differ from a plain program's by a relative error of at most 0.0053.
Values may be sent and summed in bfloat16 or wider, within the bound.
A program may use at most 192 MiB of HBM per device.

v0:
```python
import jax
import jax.numpy as jnp
from jax import lax
from jax.sharding import PartitionSpec as P

CROP = 14


highest = lax.Precision.HIGHEST


def silu_slope(values):
    sig = jax.nn.sigmoid(values)
    return sig * (1.0 + values * (1.0 - sig))


def unfold_taps(crops):
    extent = crops.shape[1]
    padded = jnp.pad(crops, ((0, 0), (1, 1), (1, 1), (0, 0)))
    pieces = [
        padded[:, offset_y : offset_y + extent, offset_x : offset_x + extent, :]
        for offset_y in range(3)
        for offset_x in range(3)
    ]
    return jnp.concatenate(pieces, axis=3)


def fold_taps(gradient_taps):
    extent = gradient_taps.shape[1]
    channels = gradient_taps.shape[3] // 9
    totals = jnp.zeros((gradient_taps.shape[0], extent + 2, extent + 2, channels), jnp.float32)
    for tap_index in range(9):
        offset_y = tap_index // 3
        offset_x = tap_index % 3
        totals = totals.at[:, offset_y : offset_y + extent, offset_x : offset_x + extent, :].add(
            gradient_taps[:, :, :, tap_index * channels : (tap_index + 1) * channels]
        )
    return totals[:, 1 : extent + 1, 1 : extent + 1, :]


def head_train(crops, classes, targets, conv_weight, deconv_weight, mask_weight):
    number = crops.shape[0]
    extent = crops.shape[1]
    channels = crops.shape[3]
    flat_count = number * extent * extent
    patches = unfold_taps(crops).reshape(flat_count, 9 * channels)
    conv_matrix = conv_weight.reshape(9 * channels, channels)
    pre_act = jnp.dot(patches, conv_matrix, preferred_element_type=jnp.float32)
    hidden = jax.nn.silu(pre_act).astype(jnp.bfloat16)
    deconv_matrix = jnp.transpose(deconv_weight, (2, 0, 1, 3)).reshape(channels, 4 * channels)
    upsampled = jnp.dot(hidden, deconv_matrix, preferred_element_type=jnp.float32)
    active = jax.nn.silu(upsampled).reshape(number, extent * extent, 4, channels)
    onehot = (
        classes[:, None] == jnp.arange(mask_weight.shape[0], dtype=jnp.int32)[None, :]
    ).astype(jnp.bfloat16)
    class_rows = jnp.dot(onehot, mask_weight, preferred_element_type=jnp.float32)
    logits = jnp.einsum("rpqc,rc->rpq", active, class_rows, precision=highest)
    labels = (
        targets.reshape(number, extent, 2, extent, 2)
        .transpose(0, 1, 3, 2, 4)
        .reshape(number, extent * extent, 4)
        .astype(jnp.float32)
    )
    losses = jnp.mean(jax.nn.softplus(logits) - labels * logits, axis=(1, 2))
    slopes = jax.nn.sigmoid(logits) - labels
    active_grad = slopes[:, :, :, None] * class_rows[:, None, None, :]
    up_grad = (active_grad.reshape(flat_count, 4 * channels) * silu_slope(upsampled)).astype(
        jnp.bfloat16
    )
    class_grad = jnp.einsum("rpq,rpqc->rc", slopes, active, precision=highest)
    grad_mask = jnp.dot(onehot.astype(jnp.float32).T, class_grad, precision=highest)
    hidden_grad = jnp.dot(up_grad, deconv_matrix.T, preferred_element_type=jnp.float32)
    pre_grad = (hidden_grad * silu_slope(pre_act)).astype(jnp.bfloat16)
    patch_grad = jnp.dot(pre_grad, conv_matrix.T, preferred_element_type=jnp.float32).reshape(
        number, extent, extent, 9 * channels
    )
    crop_grads = fold_taps(patch_grad).astype(jnp.bfloat16)
    return (losses, crop_grads, grad_mask)


def cut_crop(first_tile, second_tile, level_id, row_start, col_start):
    zero = jnp.zeros((), jnp.int32)
    first = lax.dynamic_slice(
        first_tile, (row_start, col_start, zero), (CROP, CROP, first_tile.shape[2])
    )
    second = lax.dynamic_slice(
        second_tile, (row_start, col_start, zero), (CROP, CROP, second_tile.shape[2])
    )
    return jnp.where(level_id == 0, first, second)


def on_device(
    level0,
    level1,
    conv_weight,
    deconv_weight,
    mask_weight,
    crop_level,
    crop_row,
    crop_col,
    roi_slot,
    roi_class,
    mask_target,
):
    first_tile = level0[0, 0]
    second_tile = level1[0, 0]
    levels = crop_level[0, 0]
    row_list = crop_row[0, 0]
    col_list = crop_col[0, 0]
    peers = lax.axis_size("tile")
    entries = levels.shape[0]
    per_peer = entries // peers
    channels = first_tile.shape[2]
    outgoing = jax.vmap(cut_crop, in_axes=(None, None, 0, 0, 0))(
        first_tile, second_tile, levels, row_list, col_list
    )
    outgoing = outgoing.reshape(peers, per_peer, CROP, CROP, channels)
    arrived = lax.all_to_all(outgoing, "tile", split_axis=0, concat_axis=0, tiled=True).reshape(
        entries, CROP, CROP, channels
    )
    chosen = roi_slot[0, 0]
    crops = jnp.take(arrived, chosen, axis=0)
    losses, crop_grads, grad_mask = head_train(
        crops, roi_class[0, 0], mask_target[0, 0], conv_weight, deconv_weight, mask_weight
    )
    returned = jnp.zeros((entries, CROP, CROP, channels), jnp.bfloat16).at[chosen].set(crop_grads)
    returned = returned.reshape(peers, per_peer, CROP, CROP, channels)
    back = lax.all_to_all(returned, "tile", split_axis=0, concat_axis=0, tiled=True).reshape(
        entries, CROP, CROP, channels
    )

    def place_one(position, grads_pair):
        first_all, second_all = grads_pair
        zero = jnp.zeros((), jnp.int32)
        corner = (row_list[position], col_list[position], zero)
        piece = back[position].astype(jnp.float32)
        first_old = lax.dynamic_slice(first_all, corner, piece.shape)
        first_all = lax.dynamic_update_slice(
            first_all, first_old + jnp.where(levels[position] == 0, piece, 0.0), corner
        )
        second_old = lax.dynamic_slice(second_all, corner, piece.shape)
        second_all = lax.dynamic_update_slice(
            second_all, second_old + jnp.where(levels[position] == 1, piece, 0.0), corner
        )
        return (first_all, second_all)

    start_pair = (
        jnp.zeros(first_tile.shape, jnp.float32),
        jnp.zeros(second_tile.shape, jnp.float32),
    )
    first_grads, second_grads = lax.fori_loop(
        jnp.int32(0), jnp.int32(entries), place_one, start_pair
    )
    scene_part = lax.psum_scatter(grad_mask, "tile", scatter_dimension=1, tiled=True)
    mask_part = lax.psum(scene_part, "scene")
    return (first_grads[None, None], second_grads[None, None], mask_part, losses[None, None])


def solution(mesh):
    in_specs = (
        P("scene", "tile", None, None, None),
        P("scene", "tile", None, None, None),
        P(),
        P(),
        P(),
        P("scene", "tile", None),
        P("scene", "tile", None),
        P("scene", "tile", None),
        P("scene", "tile", None),
        P("scene", "tile", None),
        P("scene", "tile", None, None, None),
    )
    out_specs = (
        P("scene", "tile", None, None, None),
        P("scene", "tile", None, None, None),
        P(None, "tile"),
        P("scene", "tile", None),
    )
    return jax.shard_map(
        on_device, mesh=mesh, in_specs=in_specs, out_specs=out_specs, check_vma=False
    )
```

profile of v0, /device:TPU:0, one launch (start us, length us, event | category | flops | bytes accessed | tf_op | source)
XLA Modules:
  0.0 827.5 jit_solution(10194169446644823317)
XLA Ops:
  9.9 83.9 %while.24 = (s32[]{:T(128)}, bf16[32,32,256]{2,1,0:T(8,128)(2,1)}, s32[24,3]{0,1:T(4,128)S(1)}, bf16[24,14,14,256]{3,2,1,0:T(8,128)(2,1)}, s32[]{:T(128)}) while((s32[]{:T(128)}, bf16[32,32,256]{2,1,0:T(8,128)(2,1)}, s32[24,3]{0,1:T(4,128)S(1)}, bf16[24,14,14,256]{3,2,1,0:T(8,128)(2,1)}, s32[]{:T(128)}) %tuple.110), condition=%wide.while_cond.9, body=%wide.while_body.9.sunk | while | flops 2 | bytes 231017 | solution.py:83
  95.6 61.6 %while.25 = (s32[]{:T(128)}, bf16[16,16,256]{2,1,0:T(8,128)(2,1)S(1)}, s32[24,3]{0,1:T(4,128)S(1)}, bf16[24,14,14,256]{3,2,1,0:T(8,128)(2,1)}, s32[]{:T(128)}) while((s32[]{:T(128)}, bf16[16,16,256]{2,1,0:T(8,128)(2,1)S(1)}, s32[24,3]{0,1:T(4,128)S(1)}, bf16[24,14,14,256]{3,2,1,0:T(8,128)(2,1)}, s32[]{:T(128)}) %tuple.109), condition=%wide.while_cond.10, body=%wide.while_body.10.sunk | while | flops 2 | bytes 216681 | solution.py:86
  157.4 4.5 broadcast_select_fusion
  161.9 6.5 all-to-all-start
  172.8 58.8 %all-to-all-done = bf16[8,3,14,14,256]{4,3,2,1,0:T(8,128)(2,1)} async-done(((bf16[8,3,14,14,256]{4,3,2,1,0:T(8,128)(2,1)}), bf16[8,3,14,14,256]{4,3,2,1,0:T(8,128)(2,1)}, u32[]{:S(2)}, u32[]{:S(2)}) %all-to-all-start) | async-done | bytes 2408480 | tf_op jit(solution)/shard_map/all_to_all | solution.py:118
  231.6 4.1 gather_fusion
  259.5 29.8 %reshape.564 = bf16[4312,2304]{1,0:T(8,128)(2,1)} reshape(bf16[22,14,14,2304]{3,2,1,0:T(8,128)(2,1)} %slice_dynamic-update-slice_fusion) | data formatting | bytes 39739392 | tf_op jit(solution)/shard_map/reshape | solution.py:46
  289.2 9.7 %fusion.47 = f32[4312,256]{1,0:T(8,128)S(1)} fusion(bf16[4312,2304]{1,0:T(8,128)(2,1)} %reshape.564, bf16[2304,256]{1,0:T(8,128)(2,1)S(1)} %bitcast.127), kind=kOutput, calls=%fused_computation.101 | convolution fusion | flops 5086642176 | bytes 25464832 | tf_op jit(solution)/shard_map/dot_general | solution.py:48
  298.9 14.4 %fusion.4 = (f32[4312,1024]{1,0:T(8,128)}, f32[4312,1024]{1,0:T(8,128)}) fusion(bf16[256,1024]{0,1:T(8,128)(2,1)S(1)} %bitcast.139, f32[4312,256]{1,0:T(8,128)S(1)} %fusion.47), kind=kOutput, calls=%fused_computation.14 | convolution fusion | flops 2283911168 | bytes 40263680 | tf_op jit(solution)/shard_map/dot_general | solution.py:51
  313.3 22.2 %reshape.567 = f32[22,196,4,256]{3,2,1,0:T(4,128)} reshape(f32[4312,1024]{1,0:T(8,128)} %get-tuple-element.216) | data formatting | bytes 35323904 | tf_op jit(solution)/shard_map/reshape | solution.py:52
  335.5 25.0 %fusion.7 = f32[22,1,196,4]{1,2,3,0:T(8,128)} fusion(f32[22,196,4,256]{3,2,1,0:T(4,128)} %reshape.567, f32[22,256,1,1]{1,0,2,3:T(8,128)S(1)} %bitcast.141), kind=kOutput, calls=%fused_computation.17 | convolution fusion | flops 52985856 | bytes 17753472 | tf_op jit(solution)/shard_map/rpqc,rc->rpq/dot_general | solution.py:57
  360.5 6.2 copy.24
  367.7 5.4 broadcast_multiply_fusion
  373.1 8.8 %copy.28 = f32[539,8,4,256]{3,1,2,0:T(8,128)} copy(f32[539,8,4,256]{3,2,1,0:T(4,128)S(1)} %bitcast.128) | data formatting | bytes 35323904
  381.9 16.4 %fusion.11 = bf16[4312,256]{1,0:T(8,128)(2,1)S(1)} fusion(bf16[256,1024]{0,1:T(8,128)(2,1)S(1)} %bitcast.140, f32[4312,1024]{1,0:T(8,128)} %bitcast.130, f32[4312,1024]{1,0:T(8,128)} %get-tuple-element.217, f32[4312,256]{1,0:T(8,128)} %copy-done.20), kind=kOutput, calls=%fused_computation.23 | convolution fusion | flops 2310404096 | bytes 42471424 | tf_op jit(solution)/shard_map/dot_general | solution.py:72
  400.4 18.6 %fusion.20 = f32[22,14,14,2304]{3,0,2,1:T(8,128)} fusion(bf16[2304,256,1,1]{1,0,3,2:T(8,128)(2,1)S(1)} %bitcast.126, bf16[22,14,14,256]{3,2,1,0:T(8,128)(2,1)} %dot_general.31), kind=kOutput, calls=%fused_computation.52 | convolution fusion | flops 5086642176 | bytes 43126784 | tf_op jit(solution)/shard_map/dot_general | solution.py:74
  422.0 5.0 fusion.19
  427.0 5.3 fusion.12
  456.8 8.1 scatter_fusion
  464.9 4.4 all-to-all-start.1
  469.4 17.3 %fusion.5 = f32[22,1,256,1]{2,1,3,0:T(1,128)S(1)} fusion(f32[22,196,4,256]{3,2,1,0:T(4,128)} %reshape.567, f32[22,196,4,1]{1,2,0,3:T(4,128)S(1)} %bitcast.137), kind=kOutput, calls=%fused_computation.15 | convolution fusion | flops 52985856 | bytes 17753472 | tf_op jit(solution)/shard_map/rpq,rpqc->rc/dot_general | solution.py:70
  488.2 37.3 %reduce-scatter.2.cloned.1.call-done = f32[80,32]{0,1:T(8,128)} async-done(((f32[80,256]{0,1:T(8,128)}), f32[80,32]{0,1:T(8,128)}) %reduce-scatter.2.cloned.1.call-update) | async-done | bytes 10256 | tf_op jit(solution)/shard_map/reduce_scatter | solution.py:154
  525.5 17.2 %psum.7 = f32[80,32]{0,1:T(8,128)} all-reduce(f32[80,32]{0,1:T(8,128)} %reduce-scatter.2.cloned.1.call-done), channel_id=1, replica_groups=mesh['scene'=4,'tile'=8] {'scene'}, use_global_device_ids=true, to_apply=%region_5.6 | all-reduce | flops 2560 | bytes 20480 | tf_op jit(solution)/shard_map/psum | solution.py:155
  542.9 276.3 %while.23 = (s32[]{:T(128)}, f32[32,32,256]{2,1,0:T(8,128)S(1)}, f32[16,16,256]{2,1,0:T(8,128)S(1)}, s32[24]{0:T(128)S(1)}, s32[24]{0:T(128)S(1)}, /*index=5*/s3...) while((s32[]{:T(128)}, f32[32,32,256]{2,1,0:T(8,128)S(1)}, ...), condition=%wide.region_3.4_spmd, body=%wide.region_2.3_spmd.sunk | while | flops 250894 | bytes 1706311 | solution.py:151
  (384 shorter events, 295.1 us)
Async XLA Ops:
  7.2 282.1 %copy-start = (bf16[3,3,256,256]{3,2,1,0:T(8,128)(2,1)S(1)}, bf16[3,3,256,256]{3,2,1,0:T(8,128)(2,1)}, u32[]{:S(2)}) copy-start(bf16[3,3,256,256]{3,2,1,0:T(8,128)(2,1)} %param.33) | copy-start | bytes 3538948
  7.2 88.4 %copy-start.4 = (bf16[1,1,16,16,256]{4,3,2,1,0:T(8,128)(2,1)S(1)}, bf16[1,1,16,16,256]{4,3,2,1,0:T(8,128)(2,1)}, u32[]{:S(2)}) copy-start(bf16[1,1,16,16,256]{4,3,2,1,0:T(8,128)(2,1)} %param.32) | copy-start | bytes 393220
  7.2 150.1 %copy-start.18 = (s32[1,1,24]{2,1,0:T(1,128)S(1)}, s32[1,1,24]{2,1,0:T(1,128)}, u32[]{:S(2)}) copy-start(s32[1,1,24]{2,1,0:T(1,128)} %param.36) | copy-start | bytes 292
  161.9 6.5 copy-start.5
  161.9 6.7 copy-start.8
  161.9 8.7 %copy-start.17 = (s32[1,1,22]{2,1,0:T(1,128)S(1)}, s32[1,1,22]{2,1,0:T(1,128)}, u32[]{:S(2)}) copy-start(s32[1,1,22]{2,1,0:T(1,128)} %param.39) | copy-start | bytes 268
  161.9 9.9 %copy-start.15 = (s32[4]{0:T(128)S(1)}, s32[4]{0:T(128)}, u32[]{:S(2)}) copy-start(s32[4]{0:T(128)} %constant.325.clone.1) | copy-start | bytes 52
  161.9 10.7 %copy-start.11 = (s32[1,1,22]{2,1,0:T(1,128)S(1)}, s32[1,1,22]{2,1,0:T(1,128)}, u32[]{:S(2)}) copy-start(s32[1,1,22]{2,1,0:T(1,128)} %param.40) | copy-start | bytes 268
  161.9 10.7 %copy-start.16 = (bf16[80,256]{1,0:T(8,128)(2,1)S(1)}, bf16[80,256]{1,0:T(8,128)(2,1)}, u32[]{:S(2)}) copy-start(bf16[80,256]{1,0:T(8,128)(2,1)} %param.35) | copy-start | bytes 122884
  161.9 69.7 %all-to-all-start = ((bf16[8,3,14,14,256]{4,3,2,1,0:T(8,128)(2,1)}), bf16[8,3,14,14,256]{4,3,2,1,0:T(8,128)(2,1)}, u32[]{:S(2)}, u32[]{:S(2)}) async-start(bf16[8,3,14,14,256]{4,3,2,1,0:T(8,128)(2,1)} %broadcast_select_fusion), calls=%async_computation | async-start | bytes 5505024 | tf_op jit(solution)/shard_map/all_to_all | solution.py:118
  168.6 130.3 %copy-start.6 = (bf16[2,2,256,256]{2,3,1,0:T(8,128)(2,1)}, bf16[2,2,256,256]{2,3,1,0:T(8,128)(2,1)S(1)}, u32[]{:S(2)}) copy-start(bf16[2,2,256,256]{2,3,1,0:T(8,128)(2,1)S(1)} %copy.16) | copy-start | bytes 1572868
  170.5 67.2 %copy-start.9 = (s32[22]{0:T(128)}, s32[22]{0:T(128)S(1)}, u32[]{:S(2)}) copy-start(s32[22]{0:T(128)S(1)} %fusion.40) | copy-start | bytes 268
  242.2 5.3 copy-start.1
  298.9 14.4 %copy-start.20 = (f32[4312,256]{1,0:T(8,128)}, f32[4312,256]{1,0:T(8,128)S(1)}, u32[]{:S(2)}) copy-start(f32[4312,256]{1,0:T(8,128)S(1)} %fusion.47) | copy-start | bytes 13246468
  373.1 8.8 %copy-start.7 = (bf16[2,2,256,256]{2,3,1,0:T(8,128)(2,1)S(1)}, bf16[2,2,256,256]{2,3,1,0:T(8,128)(2,1)}, u32[]{:S(2)}) copy-start(bf16[2,2,256,256]{2,3,1,0:T(8,128)(2,1)} %copy-done.6) | copy-start | bytes 1572868
  419.0 2.4 slice-start
  452.8 3.9 copy-start.10
  464.9 77.8 %all-to-all-start.1 = ((bf16[8,3,14,14,256]{4,3,2,1,0:T(8,128)(2,1)}), bf16[8,3,14,14,256]{4,3,2,1,0:T(8,128)(2,1)}, u32[]{:S(2)}, u32[]{:S(2)}) async-start(bf16[8,3,14,14,256]{4,3,2,1,0:T(8,128)(2,1)} %bitcast.129), calls=%async_computation.1 | async-start | bytes 5505024 | tf_op jit(solution)/shard_map/all_to_all | solution.py:128
  469.3 56.2 %reduce-scatter.2.cloned.1.call-start = ((), (), s32[]{:S(2)}) async-start(), calls=%async_computation.3 | async-start | bytes 147456 | tf_op jit(solution)/shard_map/reduce_scatter | solution.py:154
  469.4 17.3 %copy-start.12 = (s32[1,1,22]{2,1,0:T(1,128)S(1)}, s32[1,1,22]{2,1,0:T(1,128)}, u32[]{:S(2)}) copy-start(s32[1,1,22]{2,1,0:T(1,128)} %param.40) | copy-start | bytes 268
  469.4 73.5 %copy-start.13 = (s32[1,1,24]{2,1,0:T(1,128)S(1)}, s32[1,1,24]{2,1,0:T(1,128)}, u32[]{:S(2)}) copy-start(s32[1,1,24]{2,1,0:T(1,128)} %param.37) | copy-start | bytes 292
  469.4 73.5 %copy-start.14 = (s32[1,1,24]{2,1,0:T(1,128)S(1)}, s32[1,1,24]{2,1,0:T(1,128)}, u32[]{:S(2)}) copy-start(s32[1,1,24]{2,1,0:T(1,128)} %param.38) | copy-start | bytes 292
  469.4 73.5 %copy-start.19 = (s32[1,1,24]{2,1,0:T(1,128)S(1)}, s32[1,1,24]{2,1,0:T(1,128)}, u32[]{:S(2)}) copy-start(s32[1,1,24]{2,1,0:T(1,128)} %param.36) | copy-start | bytes 292
  819.2 1.0 copy-start.3
  (1 other events, 0.7 us)
Sparse Core Ops, SparseCore 0:
  487.8 37.6 reduce-scatter.1
where the time goes:
time: 843 us; the launch traced here: 827 us
  local copies, waits for them, and re-layouts  322 us (38%)
  loops' own time  193 us (23%)
  matrix products  102 us (12%)
  waiting for transfers between devices  96.1 us (11%)
  other arithmetic  71.3 us (8%)
  blocking collectives  17.2 us (2%)
  between operations  14.8 us (2%)
  starting transfers between devices  10.9 us (1%)
    another operation x1, loops' own time, on_device(): lax.fori_loop(jnp.int32(0), jnp.int32(entries), place_one, start_pair)  193 us
    gather x144, local copies, waits for them, and re-layouts  145 us
    all_to_all x1, waiting for transfers between devices, on_device(): lax.all_to_all(outgoing, 'tile', split_axis=0, concat_axis=0, tiled=True)  58.8 us
    reduce_scatter x1, waiting for transfers between devices, on_device(): lax.psum_scatter(grad_mask, 'tile', scatter_dimension=1, tiled=True)  37.3 us
    scatter-add x8, other arithmetic, fold_taps(): totals.at[:, offset_y:offset_y + extent, offset_x:offset_x + extent, :]  30.5 us
    dynamic_slice x48, local copies, waits for them, and re-layouts, place_one(): corner = (row_list[position], col_list[position], zero)  30.2 us
    reshape x1, local copies, waits for them, and re-layouts, head_train(): patches = unfold_taps(crops).reshape(flat_count, 9 * channels)  29.8 us
    unnamed x51, local copies, waits for them, and re-layouts  26.9 us
  transfers between devices with their start and end apart: 3, of which 2 were waited for; matrix products, arithmetic and copies ran while one was open for 3% of the time, Pallas kernels for 0%

commit v1 on v0

v1 whole, which is shorter than its diff:
```python
import functools

import jax
import jax.numpy as jnp
from jax import lax
from jax.experimental import pallas as pl
from jax.experimental.pallas import tpu as pltpu
from jax.sharding import PartitionSpec as P

CROP = 14
WIDE = 16
SPAN = 24
ROWS = CROP * WIDE
TAPS = 3
NT = (((1,), (1,)), ((), ()))
HAS = ((0, 1, 2), (1, 2), (0, 1))


def sigmoid(values):
    return 0.5 + 0.5 * jnp.tanh(0.5 * values)


def line_class(index):
    return 1 if index == 0 else (2 if index == CROP - 1 else 0)


def head_kernel(
    sizes,
    row_ref,
    col_ref,
    class_ref,
    tile0_ref,
    tile1_ref,
    conv_ref,
    deconv_ref,
    mask_ref,
    target_ref,
    grad0_ref,
    grad1_ref,
    gmask_ref,
    loss_ref,
    pre_all,
    sums,
    fold,
    logit_all,
    pre_scr,
):
    side0, side1, entries, base1 = sizes
    channels = conv_ref.shape[-1]
    lanes = target_ref.shape[1]
    levels = ((tile0_ref, grad0_ref, side0, 1), (tile1_ref, grad1_ref, side1, base1))

    def conv_rows(tile_ref, side, base, start, count):
        cells = count * side
        by_tap = []
        for b in range(TAPS):
            parts = []
            for a in range(TAPS):
                block = tile_ref[b, pl.ds(start + a, count)].reshape(cells, channels)
                parts.append(jnp.dot(block, conv_ref[a, b], preferred_element_type=jnp.float32))
            low = parts[0] + parts[1]
            high = parts[1] + parts[2]
            by_tap.append((low + parts[2], high, low))
        for v in range(3):
            low = by_tap[0][v] + by_tap[1][v]
            high = by_tap[1][v] + by_tap[2][v]
            full = low + by_tap[2][v]
            for u, value in enumerate((full, high, low)):
                pre_all[v, u, pl.ds(start + base, count), 0:side, :] = value.reshape(
                    count, side, channels
                )

    for tile_ref, grad_ref, side, base in levels:
        pad = pre_all.shape[3] - side
        for v in range(3):
            pre_all[v, 0, base : base + side, side:, :] = jnp.zeros(
                (side, pad, channels), jnp.float32
            )
        count = 256 // side

        def step(index, carry, tile_ref=tile_ref, side=side, base=base, count=count):
            conv_rows(tile_ref, side, base, index * count, count)
            return carry

        lax.fori_loop(0, side // count, step, 0)

    def clear(index, carry):
        sums[:, :, index] = jnp.zeros((3, 3) + sums.shape[3:], jnp.float32)
        return carry

    lax.fori_loop(0, sums.shape[2], clear, 0)
    gmask_ref[...] = jnp.zeros_like(gmask_ref)
    logit_all[...] = jnp.zeros_like(logit_all)
    lane = lax.broadcasted_iota(jnp.int32, (ROWS, lanes), 1)
    inside = lax.broadcasted_iota(jnp.int32, (ROWS, lanes), 0) % WIDE < CROP
    column = lax.broadcasted_iota(jnp.int32, (SPAN, channels), 0)

    def one_crop(entry, carry):
        kind = class_ref[entry]

        @pl.when(kind >= 0)
        def _():
            row = row_ref[entry]
            col = col_ref[entry]
            off = lax.rem(col, 8)
            near = pl.multiple_of(col - off, 8)
            first = column == off
            last = column == off + CROP - 1
            for i in range(CROP):
                v = line_class(i)
                full = pre_all[v, 0, row + i, pl.ds(near, SPAN), :]
                left = pre_all[v, 1, row + i, pl.ds(near, SPAN), :]
                right = pre_all[v, 2, row + i, pl.ds(near, SPAN), :]
                value = jnp.where(first, left, jnp.where(last, right, full))
                value = pltpu.roll(value, SPAN - off, 0)
                pre_scr[i * WIDE : (i + 1) * WIDE, :] = value[:WIDE]
            pre = pre_scr[...]
            pre_sig = sigmoid(pre)
            hidden_f = pre * pre_sig
            pre_slope = pre_sig + hidden_f * (1.0 - pre_sig)
            hidden = hidden_f.astype(jnp.bfloat16)
            class_row = mask_ref[pl.ds(kind, 1), :]
            actives = []
            slopes_up = []
            logit = jnp.zeros((ROWS, lanes), jnp.float32)
            for q in range(4):
                up = jnp.dot(hidden, deconv_ref[q], preferred_element_type=jnp.float32)
                sig = sigmoid(up)
                active = up * sig
                actives.append(active)
                slopes_up.append((sig + active * (1.0 - sig)) * class_row)
                value = jnp.sum(active * class_row, axis=1, keepdims=True)
                logit = jnp.where(lane == entry * 4 + q, value, logit)
            logit_all[...] += logit
            slope = jnp.where(inside, sigmoid(logit) - target_ref[...], 0.0)
            class_grad = jnp.zeros((1, channels), jnp.float32)
            hidden_grad = jnp.zeros((ROWS, channels), jnp.float32)
            for q in range(4):
                one = jnp.sum(
                    jnp.where(lane == entry * 4 + q, slope, 0.0), axis=1, keepdims=True
                )
                class_grad += jnp.sum(actives[q] * one, axis=0, keepdims=True)
                up_grad = (slopes_up[q] * one).astype(jnp.bfloat16)
                hidden_grad += lax.dot_general(
                    up_grad, deconv_ref[q], NT, preferred_element_type=jnp.float32
                )
            gmask_ref[pl.ds(kind, 1), :] += class_grad
            pre_grad = (hidden_grad * pre_slope).astype(jnp.bfloat16).astype(jnp.float32)
            for i in range(CROP):
                v = line_class(i)
                value = pre_grad[i * WIDE : (i + 1) * WIDE, :]
                value = jnp.concatenate(
                    [value, jnp.zeros((SPAN - WIDE, channels), jnp.float32)], axis=0
                )
                value = pltpu.roll(value, off, 0)
                parts = (
                    jnp.where(first | last, 0.0, value),
                    jnp.where(first, value, 0.0),
                    jnp.where(last, value, 0.0),
                )
                for u, (start, size) in enumerate(((0, SPAN), (0, 8), (8, SPAN - 8))):
                    place = pl.ds(pl.multiple_of(near + start, 8), size)
                    sums[v, u, row + i, place, :] += parts[u][start : start + size]

        return carry

    lax.fori_loop(0, entries, one_crop, 0)

    logit = logit_all[...]
    loss = jnp.maximum(logit, 0.0) + jnp.log1p(jnp.exp(-jnp.abs(logit)))
    loss = jnp.where(inside, loss - target_ref[...] * logit, 0.0)
    loss_ref[...] = jnp.sum(loss, axis=0, keepdims=True)

    for tile_ref, grad_ref, side, base in levels:
        count = 256 // side
        fold[...] = jnp.zeros_like(fold)

        def step(index, carry, grad_ref=grad_ref, side=side, base=base, count=count):
            cells = count * side
            start = index * count
            for b in range(TAPS):
                total = None
                for a in range(TAPS):
                    parts = [
                        sums[v, u, pl.ds(start + base + 1 - a, count), 0:side, :]
                        for v in range(3)
                        for u in range(3)
                        if a in HAS[v] and b in HAS[u]
                    ]
                    value = functools.reduce(lambda x, y: x + y, parts)
                    value = value.reshape(cells, channels).astype(jnp.bfloat16)
                    term = lax.dot_general(
                        value, conv_ref[a, b], NT, preferred_element_type=jnp.float32
                    )
                    total = term if total is None else total + term
                fold[b, 0:count, 8 : 8 + side, :] = total.reshape(count, side, channels)
            grad_ref[pl.ds(start, count)] = (
                fold[1, 0:count, 8 : 8 + side, :]
                + fold[0, 0:count, 9 : 9 + side, :]
                + fold[2, 0:count, 7 : 7 + side, :]
            )
            return carry

        lax.fori_loop(0, side // count, step, 0)


def shifted(tile):
    return jnp.stack(
        [
            jnp.pad(tile, ((1, 1), (1, 0), (0, 0)))[:, :-1],
            jnp.pad(tile, ((1, 1), (0, 0), (0, 0))),
            jnp.pad(tile, ((1, 1), (0, 1), (0, 0)))[:, 1:],
        ]
    )


def on_device(
    level0,
    level1,
    conv_weight,
    deconv_weight,
    mask_weight,
    crop_level,
    crop_row,
    crop_col,
    roi_slot,
    roi_class,
    mask_target,
):
    first_tile = level0[0, 0]
    second_tile = level1[0, 0]
    peers = lax.axis_size("tile")
    entries = crop_level.shape[2]
    per_peer = entries // peers
    channels = first_tile.shape[2]
    side0, side1 = first_tile.shape[0], second_tile.shape[0]
    base1 = side0 + 2
    height = base1 + side1 + 1
    lanes = -(-entries * 4 // 128) * 128
    classes = mask_weight.shape[0]

    slots = roi_slot[0, 0]
    number = slots.shape[0]
    here = slots[None, :] == jnp.arange(entries, dtype=jnp.int32)[:, None]
    targets = (
        mask_target[0, 0]
        .astype(jnp.bfloat16)
        .reshape(number, CROP, 2, CROP, 2)
        .transpose(0, 1, 3, 2, 4)
        .reshape(number, CROP * CROP * 4)
    )
    told = jnp.concatenate(
        [targets, (roi_class[0, 0] + 1).astype(jnp.bfloat16)[:, None]], axis=1
    )
    outgoing = jnp.dot(
        here.astype(jnp.bfloat16), told, preferred_element_type=jnp.float32
    ).astype(jnp.bfloat16)
    outgoing = outgoing.reshape(peers, per_peer, told.shape[1])
    arrived = lax.all_to_all(outgoing, "tile", split_axis=0, concat_axis=0, tiled=True).reshape(
        entries, told.shape[1]
    )
    kinds = arrived[:, -1].astype(jnp.int32) - 1
    target = arrived[:, :-1].reshape(entries, CROP, CROP, 4).transpose(1, 2, 0, 3)
    target = target.reshape(CROP, CROP, entries * 4).astype(jnp.float32)
    target = jnp.pad(target, ((0, 0), (0, WIDE - CROP), (0, lanes - entries * 4)))
    target = target.reshape(ROWS, lanes)

    level = crop_level[0, 0]
    rows = crop_row[0, 0] + jnp.where(level == 0, 1, base1)
    cols = crop_col[0, 0]

    smem = pl.BlockSpec(memory_space=pltpu.SMEM)
    vmem = pl.BlockSpec(memory_space=pltpu.VMEM)
    grad0, grad1, gmask, loss_sums = pl.pallas_call(
        functools.partial(head_kernel, (side0, side1, entries, base1)),
        out_shape=(
            jax.ShapeDtypeStruct((side0, side0, channels), jnp.float32),
            jax.ShapeDtypeStruct((side1, side1, channels), jnp.float32),
            jax.ShapeDtypeStruct((classes, channels), jnp.float32),
            jax.ShapeDtypeStruct((1, lanes), jnp.float32),
        ),
        in_specs=[smem] * 3 + [vmem] * 6,
        out_specs=(vmem,) * 4,
        scratch_shapes=[
            pltpu.VMEM((3, 3, height, side0 + 8, channels), jnp.float32),
            pltpu.VMEM((3, 3, height, side0 + 8, channels), jnp.float32),
            pltpu.VMEM((3, 256 // side1, side0 + 16, channels), jnp.float32),
            pltpu.VMEM((ROWS, lanes), jnp.float32),
            pltpu.VMEM((ROWS, channels), jnp.float32),
        ],
        compiler_params=pltpu.CompilerParams(vmem_limit_bytes=60 * 1024 * 1024),
    )(
        rows,
        cols,
        kinds,
        shifted(first_tile),
        shifted(second_tile),
        conv_weight,
        deconv_weight.reshape(4, channels, channels),
        mask_weight.astype(jnp.float32),
        target,
    )

    losses = loss_sums[0, : entries * 4].reshape(peers, per_peer, 4).sum(axis=2)
    losses = losses / (4 * CROP * CROP)
    losses = lax.all_to_all(losses, "tile", split_axis=0, concat_axis=0, tiled=True)
    losses = jnp.sum(jnp.where(here, losses.reshape(entries)[:, None], 0.0), axis=0)
    scene_part = lax.psum_scatter(gmask, "tile", scatter_dimension=1, tiled=True)
    mask_part = lax.psum(scene_part, "scene")
    return (grad0[None, None], grad1[None, None], mask_part, losses[None, None])


def solution(mesh):
    in_specs = (
        P("scene", "tile", None, None, None),
        P("scene", "tile", None, None, None),
        P(),
        P(),
        P(),
        P("scene", "tile", None),
        P("scene", "tile", None),
        P("scene", "tile", None),
        P("scene", "tile", None),
        P("scene", "tile", None),
        P("scene", "tile", None, None, None),
    )
    out_specs = (
        P("scene", "tile", None, None, None),
        P("scene", "tile", None, None, None),
        P(None, "tile"),
        P("scene", "tile", None),
    )
    return jax.shard_map(
        on_device, mesh=mesh, in_specs=in_specs, out_specs=out_specs, check_vma=False
    )
```

time: 843 us -> 116 us (0.14); the launches traced: 827 us -> 116 us
  local copies, waits for them, and re-layouts: 322 us -> 7.35 us
  loops' own time: 193 us -> 0 us
  matrix products: 102 us -> 0.27 us
  waiting for transfers between devices: 96.1 us -> 21.2 us
  other arithmetic: 71.3 us -> 7.4 us
  Pallas kernels: 0 us -> 34.1 us
    another operation x3 -> x0, loops' own time: 193 us -> none  [the longest x1 193 us: on_device(): lax.fori_loop(jnp.int32(0), jnp.int32(entries), place_one, start_pair)]
    gather x145 -> x0, local copies, waits for them, and re-layouts: 150 us -> none
    dot_general x8 -> x1, matrix products: 102 us -> 0.27 us  [on_device(): jnp.dot(here.astype(jnp.bfloat16), told, preferred_element_type=jnp.float32)]
    all_to_all x1, waiting for transfers between devices: 58.8 us -> 1.94 us  [on_device(): lax.all_to_all(outgoing, 'tile', split_axis=0, concat_axis=0, tiled=True)]
    reshape x2 -> x3, local copies, waits for them, and re-layouts: 52 us -> 0.84 us  [the longest x1 0.65 us: on_device(): outgoing = outgoing.reshape(peers, per_peer, told.shape[1])]
    dynamic_slice x72 -> x0, local copies, waits for them, and re-layouts: 44.3 us -> none  [the longest x48 30.2 us: place_one(): corner = (row_list[position], col_list[position], zero)]
    reduce_scatter x1 -> x0, waiting for transfers between devices: 37.3 us -> none  [on_device(): lax.psum_scatter(grad_mask, 'tile', scatter_dimension=1, tiled=True)]
    pallas_call x0 -> x1, Pallas kernels: none -> 34.1 us  [on_device(): pl.pallas_call(functools.partial(head_kernel, (side0, side1, entries, bas...]
  transfers between devices with their start and end apart: 3 -> 2, of which waited for: 2 -> 2; matrix products, arithmetic and copies ran while one was open for 3% -> 5% of each run, Pallas kernels for 0% -> 0%
where the time goes in v1:
time: 116 us
  Pallas kernels  34.1 us (29%)
  blocking collectives  25.1 us (22%)
  waiting for transfers between devices  21.2 us (18%)
  between operations  14.2 us (12%)
  other arithmetic  7.4 us (6%)
  local copies, waits for them, and re-layouts  7.35 us (6%)
  starting transfers between devices  6.36 us (5%)
    pallas_call x1, Pallas kernels, on_device(): pl.pallas_call(functools.partial(head_kernel, (side0, side1, entries, bas...  34.1 us
    unnamed x2, waiting for transfers between devices  19.3 us
    psum x1, blocking collectives, on_device(): mask_part = lax.psum(scene_part, 'scene')  16.6 us
    all_to_all x1, blocking collectives, on_device(): lax.all_to_all(losses, 'tile', split_axis=0, concat_axis=0, tiled=True)  8.48 us
    all_to_all x1, starting transfers between devices, on_device(): lax.all_to_all(outgoing, 'tile', split_axis=0, concat_axis=0, tiled=True)  6.33 us
    unnamed x17, local copies, waits for them, and re-layouts  3.15 us
  transfers between devices with their start and end apart: 2, of which 2 were waited for; matrix products, arithmetic and copies ran while one was open for 5% of the time, Pallas kernels for 0%

profile of v1, /device:TPU:0, one launch (start us, length us, event | category | flops | bytes accessed | tf_op | source)
XLA Modules:
  0.0 116.0 jit_solution(15980726649616589583)
XLA Ops:
  7.2 1.2 %convert_element_type.55 = bf16[1,1,22,28,28]{4,1,3,2,0:T(2,128)(2,1)S(1)} convert(s32[1,1,22,28,28]{4,1,3,2,0:T(1,128)} %param.21) | non-fusion elementwise | flops 17248 | bytes 103488 | tf_op jit(solution)/shard_map/convert_element_type | solution.py:247
  8.4 0.3 copy.53
  9.6 0.7 reshape.74
  10.2 6.3 %all-to-all-start = ((bf16[8,3,785]{2,1,0:T(4,128)(2,1)}), bf16[8,3,785]{2,1,0:T(4,128)(2,1)S(1)}, u32[]{:S(2)}, u32[]{:S(2)}) async-start(bf16[8,3,785]{2,1,0:T(4,128)(2,1)} %reshape.74), calls=%async_computation | async-start | bytes 114688 | tf_op jit(solution)/shard_map/all_to_all | solution.py:259
  16.6 0.4 fusion
  17.1 0.6 convert_element_type.61.mask_ref
  17.8 0.5 fusion.9.row_ref
  18.3 1.4 %pad_maximum_fusion.tile0_ref = bf16[3,34,32,256]{3,2,1,0:T(8,128)(2,1)} fusion(bf16[1,34,32,256]{3,2,1,0:T(8,128)(2,1)S(1)} %get-tuple-element.37, bf16[1,34,32,256]{3,2,1,0:T(8,128)(2,1)S(1)} %get-tuple-element.38, bf16[1,34,32,256]{3,2,1,0:T(8,128)(2,1)S(1)} %get-tuple-element.36), kind=kLoop, calls=%fused_computation | loop fusion | flops 1671168 | bytes 3342336 | tf_op jit(solution)/shard_map/stack | solution.py:208
  19.7 0.8 pad_maximum_fusion.1.tile1_ref
  20.5 1.9 %all-to-all-done = bf16[8,3,785]{2,1,0:T(4,128)(2,1)S(1)} async-done(((bf16[8,3,785]{2,1,0:T(4,128)(2,1)}), bf16[8,3,785]{2,1,0:T(4,128)(2,1)S(1)}, u32[]{:S(2)}, u32[]{:S(2)}) %all-to-all-start) | async-done | bytes 37712 | tf_op jit(solution)/shard_map/all_to_all | solution.py:259
  22.5 0.7 add_reduce_fusion.class_ref
  23.3 0.5 copy.58
  24.0 0.7 bitcast_convert_fusion.target_ref
  24.7 34.1 %shard_map.138 = (f32[32,32,256]{2,1,0:T(8,128)}, f32[16,16,256]{2,1,0:T(8,128)}, f32[80,256]{1,0:T(8,128)}, f32[1,128]{1,0:T(1,128)}) custom-call(s32[24]{0:T(128)} %fusion.9.row_ref, s32[24]{0:T(128)} %bitcast.52, s32[24]{0:T(128)} %add_reduce_fusion.class_ref, bf16[3,34,32,256]{3,2,1,0:T(8,128)(2,1)} %pad_maximum_fusion.tile0_ref, ...), custom_call_target="tpu_custom_call" | custom-call | tf_op jit(solution)/shard_map/pallas_call | solution.py:274
  58.8 0.7 slice_reduce_fusion
  59.6 1.6 %copy.65 = f32[80,256]{0,1:T(8,128)} copy(f32[80,256]{1,0:T(8,128)} %get-tuple-element.10) | data formatting | bytes 163840
  61.3 8.5 %all_to_all.11 = f32[8,1,3]{2,1,0:T(1,128)S(1)} all-to-all(f32[8,1,3]{2,1,0:T(1,128)S(1)} %bitcast.51), channel_id=1, replica_groups=mesh['scene'=4,'tile'=8] {'tile'}, dimensions={0} | all-to-all | bytes 192 | tf_op jit(solution)/shard_map/all_to_all | solution.py:306
  69.8 0.5 broadcast.69
  70.3 0.7 reduce.9
  71.1 0.7 select_reduce_fusion
  71.8 19.2 %reduce-scatter.4.cloned.1.call-done = f32[32,80]{1,0:T(8,128)} async-done(((f32[256,80]{1,0:T(8,128)}), f32[32,80]{1,0:T(8,128)}) %reduce-scatter.4.cloned.1.call-update) | async-done | bytes 10256
  91.0 0.8 copy.66
  91.8 16.6 %psum.7 = f32[80,32]{1,0:T(8,128)S(1)} all-reduce(f32[80,32]{1,0:T(8,128)S(1)} %copy.66), channel_id=1, replica_groups=mesh['scene'=4,'tile'=8] {'scene'}, use_global_device_ids=true, to_apply=%region_1.2 | all-reduce | flops 2560 | bytes 20480 | tf_op jit(solution)/shard_map/psum | solution.py:309
  108.4 0.7 copy.62
  (31 shorter events, 1.6 us)
Async XLA Ops:
  7.2 2.0 %copy-start.4 = (s32[1,1,22]{2,1,0:T(1,128)S(1)}, s32[1,1,22]{2,1,0:T(1,128)}, u32[]{:S(2)}) copy-start(s32[1,1,22]{2,1,0:T(1,128)} %param.20) | copy-start | bytes 268
  7.2 2.1 %copy-start.3 = (s32[1,1,22]{2,1,0:T(1,128)S(1)}, s32[1,1,22]{2,1,0:T(1,128)}, u32[]{:S(2)}) copy-start(s32[1,1,22]{2,1,0:T(1,128)} %param.19) | copy-start | bytes 268
  7.2 9.4 %copy-start = (bf16[1,1,32,32,256]{4,3,2,1,0:T(8,128)(2,1)S(1)}, bf16[1,1,32,32,256]{4,3,2,1,0:T(8,128)(2,1)}, u32[]{:S(2)}) copy-start(bf16[1,1,32,32,256]{4,3,2,1,0:T(8,128)(2,1)} %param.11) | copy-start | bytes 1572868
  8.8 8.2 %copy-start.1 = (bf16[1,1,16,16,256]{4,3,2,1,0:T(8,128)(2,1)S(1)}, bf16[1,1,16,16,256]{4,3,2,1,0:T(8,128)(2,1)}, u32[]{:S(2)}) copy-start(bf16[1,1,16,16,256]{4,3,2,1,0:T(8,128)(2,1)} %param.12) | copy-start | bytes 393220
  9.0 8.1 %copy-start.2 = (bf16[80,256]{1,0:T(8,128)(2,1)S(1)}, bf16[80,256]{1,0:T(8,128)(2,1)}, u32[]{:S(2)}) copy-start(bf16[80,256]{1,0:T(8,128)(2,1)} %param.15) | copy-start | bytes 122884
  9.0 8.8 %copy-start.5 = (s32[1,1,24]{2,1,0:T(1,128)S(1)}, s32[1,1,24]{2,1,0:T(1,128)}, u32[]{:S(2)}) copy-start(s32[1,1,24]{2,1,0:T(1,128)} %param.17) | copy-start | bytes 292
  9.0 8.8 %copy-start.6 = (s32[1,1,24]{2,1,0:T(1,128)S(1)}, s32[1,1,24]{2,1,0:T(1,128)}, u32[]{:S(2)}) copy-start(s32[1,1,24]{2,1,0:T(1,128)} %param.16) | copy-start | bytes 292
  10.2 12.2 %all-to-all-start = ((bf16[8,3,785]{2,1,0:T(4,128)(2,1)}), bf16[8,3,785]{2,1,0:T(4,128)(2,1)S(1)}, u32[]{:S(2)}, u32[]{:S(2)}) async-start(bf16[8,3,785]{2,1,0:T(4,128)(2,1)} %reshape.74), calls=%async_computation | async-start | bytes 114688 | tf_op jit(solution)/shard_map/all_to_all | solution.py:259
  16.6 74.5 %reduce-scatter.4.cloned.1.call-start = ((), (), s32[]{:S(2)}) async-start(), calls=%async_computation.3 | async-start | bytes 147456
Sparse Core Ops, SparseCore 0:
  61.4 29.5 reduce-scatter.3

commit v2 on v1

--- a/solution.py
+++ b/solution.py
@@ -12,6 +12,7 @@
 SPAN = 24
 ROWS = CROP * WIDE
 TAPS = 3
+MESH = pl.DeviceIdType.MESH
 NT = (((1,), (1,)), ((), ()))
 HAS = ((0, 1, 2), (1, 2), (0, 1))
 
@@ -37,13 +38,14 @@
     target_ref,
     grad0_ref,
     grad1_ref,
-    gmask_ref,
-    loss_ref,
+    message_ref,
     pre_all,
     sums,
     fold,
     logit_all,
     pre_scr,
+    gmask_ref,
+    turned,
 ):
     side0, side1, entries, base1 = sizes
     channels = conv_ref.shape[-1]
@@ -169,7 +171,17 @@
     logit = logit_all[...]
     loss = jnp.maximum(logit, 0.0) + jnp.log1p(jnp.exp(-jnp.abs(logit)))
     loss = jnp.where(inside, loss - target_ref[...] * logit, 0.0)
-    loss_ref[...] = jnp.sum(loss, axis=0, keepdims=True)
+    loss = jnp.sum(loss, axis=0, keepdims=True)
+    turned[...] = gmask_ref[...].T
+    peers = message_ref.shape[0]
+    share = channels // peers
+    message_ref[...] = jnp.zeros_like(message_ref)
+    for peer in range(peers):
+        message_ref[peer, 0:share, :] = turned[peer * share : (peer + 1) * share, :]
+        for part in range(lanes // 128):
+            message_ref[peer, share + part : share + part + 1, :] = loss[
+                :, part * 128 : (part + 1) * 128
+            ]
 
     for tile_ref, grad_ref, side, base in levels:
         count = 256 // side
@@ -204,6 +216,69 @@
         lax.fori_loop(0, side // count, step, 0)
 
 
+def greet(peers, scenes, me, scene):
+    barrier = pltpu.get_barrier_semaphore()
+    for step in range(1, peers):
+        pl.semaphore_signal(
+            barrier, inc=1, device_id=(scene, lax.rem(me + step, peers)), device_id_type=MESH
+        )
+    for step in range(1, scenes):
+        pl.semaphore_signal(
+            barrier, inc=1, device_id=(lax.rem(scene + step, scenes), me), device_id_type=MESH
+        )
+    pl.semaphore_wait(barrier, peers + scenes - 2)
+
+
+def total_kernel(
+    sizes, message_ref, out_ref, loss_ref, held, part, others, send1, recv1, send2, recv2
+):
+    peers, scenes, share = sizes
+    me = lax.axis_index("tile")
+    scene = lax.axis_index("scene")
+    greet(peers, scenes, me, scene)
+    copies = []
+    for step in range(1, peers):
+        peer = lax.rem(me + step, peers)
+        copy = pltpu.make_async_remote_copy(
+            src_ref=message_ref.at[peer],
+            dst_ref=held.at[step],
+            send_sem=send1.at[step],
+            recv_sem=recv1.at[step],
+            device_id=(scene, peer),
+            device_id_type=MESH,
+        )
+        copy.start()
+        copies.append(copy)
+    own = message_ref[me]
+    loss_ref[me] = own[share:]
+    total = own[:share]
+    for step in range(1, peers):
+        copies[step - 1].wait()
+        came = held[step]
+        loss_ref[lax.rem(me + peers - step, peers)] = came[share:]
+        total = total + came[:share]
+    part[...] = total
+    copies = []
+    for step in range(1, scenes):
+        copy = pltpu.make_async_remote_copy(
+            src_ref=part,
+            dst_ref=others.at[step],
+            send_sem=send2.at[step],
+            recv_sem=recv2.at[step],
+            device_id=(lax.rem(scene + step, scenes), me),
+            device_id_type=MESH,
+        )
+        copy.start()
+        copies.append(copy)
+    for copy in copies:
+        copy.wait()
+    others[0] = part[...]
+    total = others[scene]
+    for index in range(1, scenes):
+        total = total + others[lax.rem(scene + scenes - index, scenes)]
+    out_ref[...] = total
+
+
 def shifted(tile):
     return jnp.stack(
         [
@@ -271,22 +346,25 @@
 
     smem = pl.BlockSpec(memory_space=pltpu.SMEM)
     vmem = pl.BlockSpec(memory_space=pltpu.VMEM)
-    grad0, grad1, gmask, loss_sums = pl.pallas_call(
+    share = channels // peers
+    height_sent = -(-(share + lanes // 128) // 8) * 8
+    grad0, grad1, message = pl.pallas_call(
         functools.partial(head_kernel, (side0, side1, entries, base1)),
         out_shape=(
             jax.ShapeDtypeStruct((side0, side0, channels), jnp.float32),
             jax.ShapeDtypeStruct((side1, side1, channels), jnp.float32),
-            jax.ShapeDtypeStruct((classes, channels), jnp.float32),
-            jax.ShapeDtypeStruct((1, lanes), jnp.float32),
+            jax.ShapeDtypeStruct((peers, height_sent, 128), jnp.float32),
         ),
         in_specs=[smem] * 3 + [vmem] * 6,
-        out_specs=(vmem,) * 4,
+        out_specs=(vmem,) * 3,
         scratch_shapes=[
             pltpu.VMEM((3, 3, height, side0 + 8, channels), jnp.float32),
             pltpu.VMEM((3, 3, height, side0 + 8, channels), jnp.float32),
             pltpu.VMEM((3, 256 // side1, side0 + 16, channels), jnp.float32),
             pltpu.VMEM((ROWS, lanes), jnp.float32),
             pltpu.VMEM((ROWS, channels), jnp.float32),
+            pltpu.VMEM((128, channels), jnp.float32),
+            pltpu.VMEM((channels, 128), jnp.float32),
         ],
         compiler_params=pltpu.CompilerParams(vmem_limit_bytes=60 * 1024 * 1024),
     )(
@@ -301,12 +379,33 @@
         target,
     )
 
-    losses = loss_sums[0, : entries * 4].reshape(peers, per_peer, 4).sum(axis=2)
-    losses = losses / (4 * CROP * CROP)
-    losses = lax.all_to_all(losses, "tile", split_axis=0, concat_axis=0, tiled=True)
-    losses = jnp.sum(jnp.where(here, losses.reshape(entries)[:, None], 0.0), axis=0)
-    scene_part = lax.psum_scatter(gmask, "tile", scatter_dimension=1, tiled=True)
-    mask_part = lax.psum(scene_part, "scene")
+    scenes = lax.axis_size("scene")
+    gmask, loss_rows = pl.pallas_call(
+        functools.partial(total_kernel, (peers, scenes, share)),
+        out_shape=(
+            jax.ShapeDtypeStruct((share, 128), jnp.float32),
+            jax.ShapeDtypeStruct((peers, height_sent - share, 128), jnp.float32),
+        ),
+        in_specs=[vmem],
+        out_specs=(vmem,) * 2,
+        scratch_shapes=[
+            pltpu.VMEM((peers, height_sent, 128), jnp.float32),
+            pltpu.VMEM((share, 128), jnp.float32),
+            pltpu.VMEM((scenes, share, 128), jnp.float32),
+            pltpu.SemaphoreType.DMA((peers,)),
+            pltpu.SemaphoreType.DMA((peers,)),
+            pltpu.SemaphoreType.DMA((scenes,)),
+            pltpu.SemaphoreType.DMA((scenes,)),
+        ],
+        compiler_params=pltpu.CompilerParams(collective_id=1, has_side_effects=True),
+    )(message)
+    mask_part = gmask[:, :classes].T
+    loss_rows = loss_rows[:, : lanes // 128].reshape(peers, lanes)
+    losses = lax.dynamic_slice_in_dim(
+        loss_rows, lax.axis_index("tile") * (per_peer * 4), per_peer * 4, axis=1
+    )
+    losses = losses.reshape(entries, 4).sum(axis=1) / (4 * CROP * CROP)
+    losses = jnp.sum(jnp.where(here, losses[:, None], 0.0), axis=0)
     return (grad0[None, None], grad1[None, None], mask_part, losses[None, None])
 
 

time: 116 us -> 67.4 us (0.58)
  blocking collectives: 25.1 us -> 0 us
  waiting for transfers between devices: 21.2 us -> 2.01 us
  between operations: 14.2 us -> 0.8 us
  Pallas kernels: 34.1 us -> 45.8 us
  local copies, waits for them, and re-layouts: 7.35 us -> 5.09 us
    unnamed x2 -> x0, waiting for transfers between devices: 19.3 us -> none
    pallas_call x0 -> x1, Pallas kernels: none -> 17.4 us  [on_device(): pl.pallas_call(functools.partial(total_kernel, (peers, scenes, share)), o...]
    psum x1 -> x0, blocking collectives: 16.6 us -> none  [on_device(): mask_part = lax.psum(scene_part, 'scene')]
    all_to_all x1 -> x0, blocking collectives: 8.48 us -> none  [on_device(): lax.all_to_all(losses, 'tile', split_axis=0, concat_axis=0, tiled=True)]
    pallas_call x1, Pallas kernels: 34.1 us -> 28.4 us  [on_device(): pl.pallas_call(functools.partial(head_kernel, (side0, side1, entries, bas...]
    unnamed x17 -> x14, local copies, waits for them, and re-layouts: 3.15 us -> 0.04 us
    transpose x0 -> x1, local copies, waits for them, and re-layouts: none -> 1.32 us  [on_device(): mask_part = gmask[:, :classes].T]
  transfers between devices with their start and end apart: 2 -> 1, of which waited for: 2 -> 1; matrix products, arithmetic and copies ran while one was open for 5% -> 6% of each run, Pallas kernels for 0% -> 0%
where the time goes in v2:
time: 67.4 us; the launch traced here: 67.1 us
  Pallas kernels  45.8 us (68%)
  other arithmetic  6.75 us (10%)
  starting transfers between devices  6.33 us (9%)
  local copies, waits for them, and re-layouts  5.09 us (8%)
  waiting for transfers between devices  2.01 us (3%)
  between operations  0.8 us (1%)
    pallas_call x1, Pallas kernels, on_device(): pl.pallas_call(functools.partial(head_kernel, (side0, side1, entries, bas...  28.4 us
    pallas_call x1, Pallas kernels, on_device(): pl.pallas_call(functools.partial(total_kernel, (peers, scenes, share)), o...  17.4 us
    all_to_all x1, starting transfers between devices, on_device(): lax.all_to_all(outgoing, 'tile', split_axis=0, concat_axis=0, tiled=True)  6.33 us
    another operation x2, other arithmetic, shifted(): jnp.stack([jnp.pad(tile, ((1, 1), (1, 0), (0, 0)))[:, :-1], jnp.pad(tile,...  2.17 us
    all_to_all x1, waiting for transfers between devices, on_device(): lax.all_to_all(outgoing, 'tile', split_axis=0, concat_axis=0, tiled=True)  2.01 us
  transfers between devices with their start and end apart: 1, of which 1 were waited for; matrix products, arithmetic and copies ran while one was open for 6% of the time, Pallas kernels for 0%

profile of v2, /device:TPU:0, one launch (start us, length us, event | category | flops | bytes accessed | tf_op | source)
XLA Modules:
  0.0 67.1 jit_solution(4298439345582773145)
XLA Ops:
  0.7 1.2 %convert_element_type.55 = bf16[1,1,22,28,28]{4,1,3,2,0:T(2,128)(2,1)S(1)} convert(s32[1,1,22,28,28]{4,1,3,2,0:T(1,128)} %param.21) | non-fusion elementwise | flops 17248 | bytes 103488 | tf_op jit(solution)/shard_map/convert_element_type | solution.py:322
  1.9 0.3 copy.41
  2.3 0.1 copy.42
  2.5 0.1 copy.43
  2.8 0.3 convolution_convert_fusion
  3.0 0.7 reshape.70
  3.7 6.3 %all-to-all-start = ((bf16[8,3,785]{2,1,0:T(4,128)(2,1)}), bf16[8,3,785]{2,1,0:T(4,128)(2,1)S(1)}, u32[]{:S(2)}, u32[]{:S(2)}) async-start(bf16[8,3,785]{2,1,0:T(4,128)(2,1)} %reshape.70), calls=%async_computation | async-start | bytes 114688 | tf_op jit(solution)/shard_map/all_to_all | solution.py:334
  10.0 0.4 fusion
  10.5 0.6 convert_element_type.61.mask_ref
  11.2 0.5 fusion.9.row_ref
  11.7 1.4 %pad_maximum_fusion.tile0_ref = bf16[3,34,32,256]{3,2,1,0:T(8,128)(2,1)} fusion(bf16[1,34,32,256]{3,2,1,0:T(8,128)(2,1)S(1)} %get-tuple-element.15, bf16[1,34,32,256]{3,2,1,0:T(8,128)(2,1)S(1)} %get-tuple-element.16, bf16[1,34,32,256]{3,2,1,0:T(8,128)(2,1)S(1)} %get-tuple-element.14), kind=kLoop, calls=%fused_computation | loop fusion | flops 1671168 | bytes 3342336 | tf_op jit(solution)/shard_map/stack | solution.py:283
  13.1 0.8 %pad_maximum_fusion.1.tile1_ref = bf16[3,18,16,256]{3,2,1,0:T(8,128)(2,1)} fusion(bf16[1,18,16,256]{3,2,1,0:T(8,128)(2,1)S(1)} %get-tuple-element.18, bf16[1,18,16,256]{3,2,1,0:T(8,128)(2,1)S(1)} %get-tuple-element.19, bf16[1,18,16,256]{3,2,1,0:T(8,128)(2,1)S(1)} %get-tuple-element.17), kind=kLoop, calls=%fused_computation.7 | loop fusion | flops 442368 | bytes 884736 | tf_op jit(solution)/shard_map/stack | solution.py:283
  13.9 2.0 %all-to-all-done = bf16[8,3,785]{2,1,0:T(4,128)(2,1)S(1)} async-done(((bf16[8,3,785]{2,1,0:T(4,128)(2,1)}), bf16[8,3,785]{2,1,0:T(4,128)(2,1)S(1)}, u32[]{:S(2)}, u32[]{:S(2)}) %all-to-all-start) | async-done | bytes 37712 | tf_op jit(solution)/shard_map/all_to_all | solution.py:334
  15.9 0.7 %add_reduce_fusion.class_ref = s32[24]{0:T(128)} fusion(bf16[24,785]{1,0:T(8,128)(2,1)S(1)} %reshape.71), kind=kLoop, calls=%fused_computation.19 | loop fusion | flops 48 | bytes 144 | tf_op jit(solution)/shard_map/sub | solution.py:337
  16.6 0.2 copy.45
  16.8 0.5 copy.46
  17.3 0.2 copy.47
  17.5 0.7 bitcast_convert_fusion.target_ref
  18.2 28.4 %shard_map.138 = (f32[32,32,256]{2,1,0:T(8,128)}, f32[16,16,256]{2,1,0:T(8,128)}, f32[8,40,128]{2,1,0:T(8,128)}) custom-call(s32[24]{0:T(128)} %fusion.9.row_ref, s32[24]{0:T(128)} %bitcast.46, s32[24]{0:T(128)} %add_reduce_fusion.class_ref, bf16[3,34,32,256]{3,2,1,0:T(8,128)(2,1)} %pad_maximum_fusion.tile0_ref, ...), custom_call_target="tpu_custom_call" | custom-call | tf_op jit(solution)/shard_map/pallas_call | solution.py:351
  46.5 17.4 %shard_map.139 = (f32[32,128]{1,0:T(8,128)}, f32[8,8,128]{2,1,0:T(8,128)}) custom-call(f32[8,40,128]{2,1,0:T(8,128)} %get-tuple-element.11.message_ref), custom_call_target="tpu_custom_call" | custom-call | tf_op jit(solution)/shard_map/pallas_call | solution.py:383
  64.0 0.8 %slice.31 = f32[8,1,128]{2,1,0:T(1,128)S(1)} slice(f32[8,8,128]{2,1,0:T(8,128)} %get-tuple-element.13), slice={[0:8], [0:1], [0:128]} | slice | bytes 8192 | tf_op jit(solution)/shard_map/slice | solution.py:403
  64.9 0.1 reduce_sum.18
  65.0 0.7 %select_reduce_fusion = f32[22]{0:T(128)} fusion(f32[24]{0:T(128)S(1)} %broadcast_multiply_fusion, s32[22]{0:T(128)S(1)} %bitcast.48), kind=kLoop, calls=%fused_computation.18 | loop fusion | flops 1562 | bytes 272 | tf_op jit(solution)/shard_map/reduce_sum | solution.py:408
  65.7 1.3 %slice_bitcast_fusion = f32[80,32]{0,1:T(8,128)} fusion(f32[32,128]{1,0:T(8,128)} %get-tuple-element.12), kind=kLoop, calls=%fused_computation.17 | loop fusion | bytes 20480 | tf_op jit(solution)/shard_map/transpose | solution.py:402
  (23 shorter events, 0.5 us)
Async XLA Ops:
  0.6 2.0 %copy-start.4 = (s32[1,1,22]{2,1,0:T(1,128)S(1)}, s32[1,1,22]{2,1,0:T(1,128)}, u32[]{:S(2)}) copy-start(s32[1,1,22]{2,1,0:T(1,128)} %param.20) | copy-start | bytes 268
  0.6 2.1 %copy-start.3 = (s32[1,1,22]{2,1,0:T(1,128)S(1)}, s32[1,1,22]{2,1,0:T(1,128)}, u32[]{:S(2)}) copy-start(s32[1,1,22]{2,1,0:T(1,128)} %param.19) | copy-start | bytes 268
  0.7 9.4 %copy-start = (bf16[1,1,32,32,256]{4,3,2,1,0:T(8,128)(2,1)S(1)}, bf16[1,1,32,32,256]{4,3,2,1,0:T(8,128)(2,1)}, u32[]{:S(2)}) copy-start(bf16[1,1,32,32,256]{4,3,2,1,0:T(8,128)(2,1)} %param.11) | copy-start | bytes 1572868
  2.3 8.2 %copy-start.1 = (bf16[1,1,16,16,256]{4,3,2,1,0:T(8,128)(2,1)S(1)}, bf16[1,1,16,16,256]{4,3,2,1,0:T(8,128)(2,1)}, u32[]{:S(2)}) copy-start(bf16[1,1,16,16,256]{4,3,2,1,0:T(8,128)(2,1)} %param.12) | copy-start | bytes 393220
  2.5 8.1 %copy-start.2 = (bf16[80,256]{1,0:T(8,128)(2,1)S(1)}, bf16[80,256]{1,0:T(8,128)(2,1)}, u32[]{:S(2)}) copy-start(bf16[80,256]{1,0:T(8,128)(2,1)} %param.15) | copy-start | bytes 122884
  2.6 8.6 %copy-start.5 = (s32[1,1,24]{2,1,0:T(1,128)S(1)}, s32[1,1,24]{2,1,0:T(1,128)}, u32[]{:S(2)}) copy-start(s32[1,1,24]{2,1,0:T(1,128)} %param.17) | copy-start | bytes 292
  2.6 8.6 %copy-start.6 = (s32[1,1,24]{2,1,0:T(1,128)S(1)}, s32[1,1,24]{2,1,0:T(1,128)}, u32[]{:S(2)}) copy-start(s32[1,1,24]{2,1,0:T(1,128)} %param.16) | copy-start | bytes 292
  3.7 12.2 %all-to-all-start = ((bf16[8,3,785]{2,1,0:T(4,128)(2,1)}), bf16[8,3,785]{2,1,0:T(4,128)(2,1)S(1)}, u32[]{:S(2)}, u32[]{:S(2)}) async-start(bf16[8,3,785]{2,1,0:T(4,128)(2,1)} %reshape.70), calls=%async_computation | async-start | bytes 114688 | tf_op jit(solution)/shard_map/all_to_all | solution.py:334

commit v3 on v2

--- a/solution.py
+++ b/solution.py
@@ -9,7 +9,7 @@
 
 CROP = 14
 WIDE = 16
-SPAN = 24
+GROUP = 4
 ROWS = CROP * WIDE
 TAPS = 3
 MESH = pl.DeviceIdType.MESH
@@ -52,6 +52,8 @@
     lanes = target_ref.shape[1]
     levels = ((tile0_ref, grad0_ref, side0, 1), (tile1_ref, grad1_ref, side1, base1))
 
+    halves = channels // 128
+
     def conv_rows(tile_ref, side, base, start, count):
         cells = count * side
         by_tap = []
@@ -68,15 +70,15 @@
             high = by_tap[1][v] + by_tap[2][v]
             full = low + by_tap[2][v]
             for u, value in enumerate((full, high, low)):
-                pre_all[v, u, pl.ds(start + base, count), 0:side, :] = value.reshape(
-                    count, side, channels
-                )
+                for half in range(halves):
+                    pre_all[v, u, half, pl.ds(start + base, count), 0:side, :] = value[
+                        :, half * 128 : (half + 1) * 128
+                    ].reshape(count, side, 128)
 
     for tile_ref, grad_ref, side, base in levels:
-        pad = pre_all.shape[3] - side
         for v in range(3):
-            pre_all[v, 0, base : base + side, side:, :] = jnp.zeros(
-                (side, pad, channels), jnp.float32
+            pre_all[v, 0, :, base : base + side, side : side + 8, :] = jnp.zeros(
+                (halves, side, 8, 128), jnp.float32
             )
         count = 256 // side
 
@@ -86,87 +88,102 @@
 
         lax.fori_loop(0, side // count, step, 0)
 
-    def clear(index, carry):
-        sums[:, :, index] = jnp.zeros((3, 3) + sums.shape[3:], jnp.float32)
-        return carry
-
-    lax.fori_loop(0, sums.shape[2], clear, 0)
+    for tile_ref, grad_ref, side, base in levels:
+
+        def clear(index, carry, side=side, base=base):
+            sums[:, :, :, base - 1 + index, 0:side, :] = jnp.zeros(
+                (3, 3, halves, side, 128), jnp.float32
+            )
+            return carry
+
+        lax.fori_loop(0, side + 2, clear, 0)
     gmask_ref[...] = jnp.zeros_like(gmask_ref)
     logit_all[...] = jnp.zeros_like(logit_all)
     lane = lax.broadcasted_iota(jnp.int32, (ROWS, lanes), 1)
     inside = lax.broadcasted_iota(jnp.int32, (ROWS, lanes), 0) % WIDE < CROP
-    column = lax.broadcasted_iota(jnp.int32, (SPAN, channels), 0)
-
-    def one_crop(entry, carry):
-        kind = class_ref[entry]
-
-        @pl.when(kind >= 0)
-        def _():
-            row = row_ref[entry]
-            col = col_ref[entry]
-            off = lax.rem(col, 8)
-            near = pl.multiple_of(col - off, 8)
-            first = column == off
-            last = column == off + CROP - 1
+    first = lax.broadcasted_iota(jnp.int32, (8, 128), 0) == 0
+    last = lax.broadcasted_iota(jnp.int32, (8, 128), 0) == CROP - 1 - 8
+
+    def some_crops(group, carry):
+        crops = [group * GROUP + k for k in range(GROUP)]
+        kinds = [class_ref[entry] for entry in crops]
+        rows = [row_ref[entry] for entry in crops]
+        cols = [col_ref[entry] for entry in crops]
+        class_rows = [mask_ref[pl.ds(jnp.maximum(kind, 0), 1), :] for kind in kinds]
+        slopes = []
+        hiddens = []
+        for k in range(GROUP):
             for i in range(CROP):
                 v = line_class(i)
-                full = pre_all[v, 0, row + i, pl.ds(near, SPAN), :]
-                left = pre_all[v, 1, row + i, pl.ds(near, SPAN), :]
-                right = pre_all[v, 2, row + i, pl.ds(near, SPAN), :]
-                value = jnp.where(first, left, jnp.where(last, right, full))
-                value = pltpu.roll(value, SPAN - off, 0)
-                pre_scr[i * WIDE : (i + 1) * WIDE, :] = value[:WIDE]
-            pre = pre_scr[...]
-            pre_sig = sigmoid(pre)
-            hidden_f = pre * pre_sig
-            pre_slope = pre_sig + hidden_f * (1.0 - pre_sig)
-            hidden = hidden_f.astype(jnp.bfloat16)
-            class_row = mask_ref[pl.ds(kind, 1), :]
-            actives = []
-            slopes_up = []
-            logit = jnp.zeros((ROWS, lanes), jnp.float32)
-            for q in range(4):
-                up = jnp.dot(hidden, deconv_ref[q], preferred_element_type=jnp.float32)
-                sig = sigmoid(up)
-                active = up * sig
-                actives.append(active)
-                slopes_up.append((sig + active * (1.0 - sig)) * class_row)
-                value = jnp.sum(active * class_row, axis=1, keepdims=True)
-                logit = jnp.where(lane == entry * 4 + q, value, logit)
-            logit_all[...] += logit
-            slope = jnp.where(inside, sigmoid(logit) - target_ref[...], 0.0)
-            class_grad = jnp.zeros((1, channels), jnp.float32)
-            hidden_grad = jnp.zeros((ROWS, channels), jnp.float32)
-            for q in range(4):
+                row = rows[k] + i
+                for half in range(halves):
+                    near, far = pl.ds(cols[k], 8), pl.ds(cols[k] + 8, 8)
+                    width = slice(half * 128, (half + 1) * 128)
+                    pre_scr[k, i * WIDE : i * WIDE + 8, width] = jnp.where(
+                        first,
+                        pre_all[v, 1, half, row, near, :],
+                        pre_all[v, 0, half, row, near, :],
+                    )
+                    pre_scr[k, i * WIDE + 8 : (i + 1) * WIDE, width] = jnp.where(
+                        last,
+                        pre_all[v, 2, half, row, far, :],
+                        pre_all[v, 0, half, row, far, :],
+                    )
+            pre = pre_scr[k]
+            turn = jnp.tanh(pre)
+            hidden = pre + pre * turn
+            slopes.append(0.25 * ((1.0 + turn) + hidden * (1.0 - turn)))
+            hiddens.append((0.5 * hidden).astype(jnp.bfloat16))
+        actives = [[] for _ in crops]
+        bends = [[] for _ in crops]
+        logits = [jnp.zeros((ROWS, lanes), jnp.float32) for _ in crops]
+        for q in range(4):
+            for k, entry in enumerate(crops):
+                up = jnp.dot(hiddens[k], deconv_ref[q], preferred_element_type=jnp.float32)
+                turn = jnp.tanh(up)
+                active = up + up * turn
+                actives[k].append(active)
+                bends[k].append(((1.0 + turn) + active * (1.0 - turn)) * class_rows[k])
+                value = jnp.sum(active * class_rows[k], axis=1, keepdims=True)
+                logits[k] = jnp.where(lane == entry * 4 + q, value, logits[k])
+        steep = []
+        for k in range(GROUP):
+            logit_all[...] += logits[k]
+            steep.append(
+                jnp.where(
+                    inside & (kinds[k] >= 0), sigmoid(logits[k]) - target_ref[...], 0.0
+                )
+            )
+        class_grads = [jnp.zeros((1, channels), jnp.float32) for _ in crops]
+        hidden_grads = [jnp.zeros((ROWS, channels), jnp.float32) for _ in crops]
+        for q in range(4):
+            for k, entry in enumerate(crops):
                 one = jnp.sum(
-                    jnp.where(lane == entry * 4 + q, slope, 0.0), axis=1, keepdims=True
+                    jnp.where(lane == entry * 4 + q, steep[k], 0.0), axis=1, keepdims=True
                 )
-                class_grad += jnp.sum(actives[q] * one, axis=0, keepdims=True)
-                up_grad = (slopes_up[q] * one).astype(jnp.bfloat16)
-                hidden_grad += lax.dot_general(
+                class_grads[k] += jnp.sum(actives[k][q] * one, axis=0, keepdims=True)
+                up_grad = (bends[k][q] * one).astype(jnp.bfloat16)
+                hidden_grads[k] += lax.dot_general(
                     up_grad, deconv_ref[q], NT, preferred_element_type=jnp.float32
                 )
-            gmask_ref[pl.ds(kind, 1), :] += class_grad
-            pre_grad = (hidden_grad * pre_slope).astype(jnp.bfloat16).astype(jnp.float32)
+        for k in range(GROUP):
+            gmask_ref[pl.ds(jnp.maximum(kinds[k], 0), 1), :] += class_grads[k]
+            pre_grad = (hidden_grads[k] * slopes[k]).astype(jnp.bfloat16).astype(jnp.float32)
             for i in range(CROP):
                 v = line_class(i)
-                value = pre_grad[i * WIDE : (i + 1) * WIDE, :]
-                value = jnp.concatenate(
-                    [value, jnp.zeros((SPAN - WIDE, channels), jnp.float32)], axis=0
-                )
-                value = pltpu.roll(value, off, 0)
-                parts = (
-                    jnp.where(first | last, 0.0, value),
-                    jnp.where(first, value, 0.0),
-                    jnp.where(last, value, 0.0),
-                )
-                for u, (start, size) in enumerate(((0, SPAN), (0, 8), (8, SPAN - 8))):
-                    place = pl.ds(pl.multiple_of(near + start, 8), size)
-                    sums[v, u, row + i, place, :] += parts[u][start : start + size]
-
+                row = rows[k] + i
+                for half in range(halves):
+                    near, far = pl.ds(cols[k], 8), pl.ds(cols[k] + 8, 8)
+                    width = slice(half * 128, (half + 1) * 128)
+                    value = pre_grad[i * WIDE : i * WIDE + 8, width]
+                    sums[v, 0, half, row, near, :] += jnp.where(first, 0.0, value)
+                    sums[v, 1, half, row, near, :] += jnp.where(first, value, 0.0)
+                    value = pre_grad[i * WIDE + 8 : (i + 1) * WIDE, width]
+                    sums[v, 0, half, row, far, :] += jnp.where(last, 0.0, value)
+                    sums[v, 2, half, row, far, :] += jnp.where(last, value, 0.0)
         return carry
 
-    lax.fori_loop(0, entries, one_crop, 0)
+    lax.fori_loop(0, entries // GROUP, some_crops, 0)
 
     logit = logit_all[...]
     loss = jnp.maximum(logit, 0.0) + jnp.log1p(jnp.exp(-jnp.abs(logit)))
@@ -190,22 +207,33 @@
         def step(index, carry, grad_ref=grad_ref, side=side, base=base, count=count):
             cells = count * side
             start = index * count
+            totals = [None] * TAPS
+            for a in range(TAPS):
+                values = [[] for _ in range(TAPS)]
+                for half in range(halves):
+                    by_tap = [None] * TAPS
+                    for v in range(3):
+                        if a not in HAS[v]:
+                            continue
+                        place = pl.ds(start + base + 1 - a, count)
+                        full, left, right = (
+                            sums[v, u, half, place, 0:side, :] for u in range(3)
+                        )
+                        low = full + right
+                        for b, value in enumerate((low, low + left, full + left)):
+                            by_tap[b] = value if by_tap[b] is None else by_tap[b] + value
+                    for b in range(TAPS):
+                        values[b].append(by_tap[b].reshape(cells, 128).astype(jnp.bfloat16))
+                for b in range(TAPS):
+                    term = lax.dot_general(
+                        jnp.concatenate(values[b], axis=1),
+                        conv_ref[a, b],
+                        NT,
+                        preferred_element_type=jnp.float32,
+                    )
+                    totals[b] = term if totals[b] is None else totals[b] + term
             for b in range(TAPS):
-                total = None
-                for a in range(TAPS):
-                    parts = [
-                        sums[v, u, pl.ds(start + base + 1 - a, count), 0:side, :]
-                        for v in range(3)
-                        for u in range(3)
-                        if a in HAS[v] and b in HAS[u]
-                    ]
-                    value = functools.reduce(lambda x, y: x + y, parts)
-                    value = value.reshape(cells, channels).astype(jnp.bfloat16)
-                    term = lax.dot_general(
-                        value, conv_ref[a, b], NT, preferred_element_type=jnp.float32
-                    )
-                    total = term if total is None else total + term
-                fold[b, 0:count, 8 : 8 + side, :] = total.reshape(count, side, channels)
+                fold[b, 0:count, 8 : 8 + side, :] = totals[b].reshape(count, side, channels)
             grad_ref[pl.ds(start, count)] = (
                 fold[1, 0:count, 8 : 8 + side, :]
                 + fold[0, 0:count, 9 : 9 + side, :]
@@ -280,6 +308,7 @@
 
 
 def shifted(tile):
+    tile = tile * 0.5
     return jnp.stack(
         [
             jnp.pad(tile, ((1, 1), (1, 0), (0, 0)))[:, :-1],
@@ -358,11 +387,11 @@
         in_specs=[smem] * 3 + [vmem] * 6,
         out_specs=(vmem,) * 3,
         scratch_shapes=[
-            pltpu.VMEM((3, 3, height, side0 + 8, channels), jnp.float32),
-            pltpu.VMEM((3, 3, height, side0 + 8, channels), jnp.float32),
+            pltpu.VMEM((3, 3, channels // 128, height, side0 + 8, 128), jnp.float32),
+            pltpu.VMEM((3, 3, channels // 128, height, side0 + 8, 128), jnp.float32),
             pltpu.VMEM((3, 256 // side1, side0 + 16, channels), jnp.float32),
             pltpu.VMEM((ROWS, lanes), jnp.float32),
-            pltpu.VMEM((ROWS, channels), jnp.float32),
+            pltpu.VMEM((GROUP, ROWS, channels), jnp.float32),
             pltpu.VMEM((128, channels), jnp.float32),
             pltpu.VMEM((channels, 128), jnp.float32),
         ],

time: 67.4 us -> 60.4 us (0.90)
  Pallas kernels: 45.8 us -> 38.6 us
    pallas_call x1, Pallas kernels: 17.4 us -> 11.8 us  [on_device(): pl.pallas_call(functools.partial(total_kernel, (peers, scenes, share)), o...]
    pallas_call x1, Pallas kernels: 28.4 us -> 26.8 us  [on_device(): pl.pallas_call(functools.partial(head_kernel, (side0, side1, entries, bas...]
where the time goes in v3:
time: 60.4 us; the launch traced here: 59.9 us
  Pallas kernels  38.6 us (64%)
  other arithmetic  6.81 us (11%)
  starting transfers between devices  6.46 us (11%)
  local copies, waits for them, and re-layouts  5.29 us (9%)
  waiting for transfers between devices  1.7 us (3%)
  between operations  0.8 us (1%)
    pallas_call x1, Pallas kernels, on_device(): pl.pallas_call(functools.partial(head_kernel, (side0, side1, entries, bas...  26.8 us
    pallas_call x1, Pallas kernels, on_device(): pl.pallas_call(functools.partial(total_kernel, (peers, scenes, share)), o...  11.8 us
    all_to_all x1, starting transfers between devices, on_device(): lax.all_to_all(outgoing, 'tile', split_axis=0, concat_axis=0, tiled=True)  6.46 us
    another operation x2, other arithmetic, shifted(): jnp.stack([jnp.pad(tile, ((1, 1), (1, 0), (0, 0)))[:, :-1], jnp.pad(tile,...  2.17 us
    all_to_all x1, waiting for transfers between devices, on_device(): lax.all_to_all(outgoing, 'tile', split_axis=0, concat_axis=0, tiled=True)  1.7 us
    transpose x1, local copies, waits for them, and re-layouts, on_device(): mask_part = gmask[:, :classes].T  1.32 us
    convert_element_type x1, other arithmetic, on_device(): targets = mask_target[0, 0].astype(jnp.bfloat16).reshape(number, CROP, 2,...  1.25 us
  transfers between devices with their start and end apart: 1, of which 1 were waited for; matrix products, arithmetic and copies ran while one was open for 6% of the time, Pallas kernels for 0%

profile of v3, /device:TPU:0, one launch (start us, length us, event | category | flops | bytes accessed | tf_op | source)
XLA Modules:
  0.0 59.9 jit_solution(15298362439074117598)
XLA Ops:
  0.7 1.2 %convert_element_type.55 = bf16[1,1,22,28,28]{4,1,3,2,0:T(2,128)(2,1)S(1)} convert(s32[1,1,22,28,28]{4,1,3,2,0:T(1,128)} %param.21) | non-fusion elementwise | flops 17248 | bytes 103488 | tf_op jit(solution)/shard_map/convert_element_type | solution.py:351
  1.9 0.3 copy.41
  2.3 0.1 copy.42
  2.4 0.1 copy.43
  2.7 0.3 convolution_convert_fusion
  3.0 0.7 %reshape.74 = bf16[8,3,785]{2,1,0:T(4,128)(2,1)} reshape(bf16[24,785]{1,0:T(8,128)(2,1)S(1)} %convolution_convert_fusion) | data formatting | bytes 75360 | tf_op jit(solution)/shard_map/reshape | solution.py:362
  3.6 6.5 %all-to-all-start = ((bf16[8,3,785]{2,1,0:T(4,128)(2,1)}), bf16[8,3,785]{2,1,0:T(4,128)(2,1)S(1)}, u32[]{:S(2)}, u32[]{:S(2)}) async-start(bf16[8,3,785]{2,1,0:T(4,128)(2,1)} %reshape.74), calls=%async_computation | async-start | bytes 114688 | tf_op jit(solution)/shard_map/all_to_all | solution.py:363
  10.2 0.4 fusion
  10.8 0.2 copy-done.2
  10.9 0.6 %convert_element_type.61.mask_ref = f32[80,256]{1,0:T(8,128)} convert(bf16[80,256]{1,0:T(8,128)(2,1)S(1)} %copy-done.2) | non-fusion elementwise | flops 20480 | bytes 122880 | tf_op jit(solution)/shard_map/convert_element_type | solution.py:407
  11.6 0.5 fusion.9.row_ref
  12.1 1.4 %pad_maximum_fusion.tile0_ref = bf16[3,34,32,256]{3,2,1,0:T(8,128)(2,1)} fusion(bf16[1,34,32,256]{3,2,1,0:T(8,128)(2,1)S(1)} %get-tuple-element.15, bf16[1,34,32,256]{3,2,1,0:T(8,128)(2,1)S(1)} %get-tuple-element.16, bf16[1,34,32,256]{3,2,1,0:T(8,128)(2,1)S(1)} %get-tuple-element.14), kind=kLoop, calls=%fused_computation | loop fusion | flops 1671168 | bytes 3342336 | tf_op jit(solution)/shard_map/stack | solution.py:312
  13.5 0.8 %pad_maximum_fusion.1.tile1_ref = bf16[3,18,16,256]{3,2,1,0:T(8,128)(2,1)} fusion(bf16[1,18,16,256]{3,2,1,0:T(8,128)(2,1)S(1)} %get-tuple-element.18, bf16[1,18,16,256]{3,2,1,0:T(8,128)(2,1)S(1)} %get-tuple-element.19, bf16[1,18,16,256]{3,2,1,0:T(8,128)(2,1)S(1)} %get-tuple-element.17), kind=kLoop, calls=%fused_computation.8 | loop fusion | flops 442368 | bytes 884736 | tf_op jit(solution)/shard_map/stack | solution.py:312
  14.3 1.7 %all-to-all-done = bf16[8,3,785]{2,1,0:T(4,128)(2,1)S(1)} async-done(((bf16[8,3,785]{2,1,0:T(4,128)(2,1)}), bf16[8,3,785]{2,1,0:T(4,128)(2,1)S(1)}, u32[]{:S(2)}, u32[]{:S(2)}) %all-to-all-start) | async-done | bytes 37712 | tf_op jit(solution)/shard_map/all_to_all | solution.py:363
  16.0 0.7 %add_reduce_fusion.class_ref = s32[24]{0:T(128)} fusion(bf16[24,785]{1,0:T(8,128)(2,1)S(1)} %reshape.75), kind=kLoop, calls=%fused_computation.21 | loop fusion | flops 48 | bytes 144 | tf_op jit(solution)/shard_map/sub | solution.py:366
  16.7 0.2 copy.45
  16.9 0.5 copy.46
  17.4 0.2 copy.47
  17.6 0.7 %bitcast_convert_fusion.target_ref = f32[224,128]{1,0:T(8,128)} fusion(bf16[14,16,128]{2,1,0:T(8,128)(2,1)S(1)} %pad.35), kind=kLoop, calls=%fused_computation.15 | loop fusion | flops 28672 | bytes 172032 | tf_op jit(solution)/shard_map/reshape | solution.py:370
  18.3 26.8 %shard_map.138 = (f32[32,32,256]{2,1,0:T(8,128)}, f32[16,16,256]{2,1,0:T(8,128)}, f32[8,40,128]{2,1,0:T(8,128)}) custom-call(s32[24]{0:T(128)} %fusion.9.row_ref, s32[24]{0:T(128)} %bitcast.46, s32[24]{0:T(128)} %add_reduce_fusion.class_ref, bf16[3,34,32,256]{3,2,1,0:T(8,128)(2,1)} %pad_maximum_fusion.tile0_ref, ...), custom_call_target="tpu_custom_call" | custom-call | tf_op jit(solution)/shard_map/pallas_call | solution.py:380
  45.1 11.8 %shard_map.139 = (f32[32,128]{1,0:T(8,128)}, f32[8,8,128]{2,1,0:T(8,128)}) custom-call(f32[8,40,128]{2,1,0:T(8,128)} %get-tuple-element.11.message_ref), custom_call_target="tpu_custom_call" | custom-call | tf_op jit(solution)/shard_map/pallas_call | solution.py:412
  56.8 0.8 %slice.31 = f32[8,1,128]{2,1,0:T(1,128)S(1)} slice(f32[8,8,128]{2,1,0:T(8,128)} %get-tuple-element.13), slice={[0:8], [0:1], [0:128]} | slice | bytes 8192 | tf_op jit(solution)/shard_map/slice | solution.py:432
  57.9 0.7 %select_reduce_fusion = f32[22]{0:T(128)} fusion(f32[24]{0:T(128)S(1)} %broadcast_multiply_fusion, s32[22]{0:T(128)S(1)} %bitcast.48), kind=kLoop, calls=%fused_computation.20 | loop fusion | flops 1562 | bytes 272 | tf_op jit(solution)/shard_map/reduce_sum | solution.py:437
  58.6 1.3 %slice_bitcast_fusion = f32[80,32]{0,1:T(8,128)} fusion(f32[32,128]{1,0:T(8,128)} %get-tuple-element.12), kind=kLoop, calls=%fused_computation.19 | loop fusion | bytes 20480 | tf_op jit(solution)/shard_map/transpose | solution.py:431
  (25 shorter events, 0.7 us)
Async XLA Ops:
  0.6 2.0 %copy-start.4 = (s32[1,1,22]{2,1,0:T(1,128)S(1)}, s32[1,1,22]{2,1,0:T(1,128)}, u32[]{:S(2)}) copy-start(s32[1,1,22]{2,1,0:T(1,128)} %param.20) | copy-start | bytes 268
  0.6 2.1 %copy-start.3 = (s32[1,1,22]{2,1,0:T(1,128)S(1)}, s32[1,1,22]{2,1,0:T(1,128)}, u32[]{:S(2)}) copy-start(s32[1,1,22]{2,1,0:T(1,128)} %param.19) | copy-start | bytes 268
  0.7 9.5 %copy-start = (bf16[1,1,32,32,256]{4,3,2,1,0:T(8,128)(2,1)S(1)}, bf16[1,1,32,32,256]{4,3,2,1,0:T(8,128)(2,1)}, u32[]{:S(2)}) copy-start(bf16[1,1,32,32,256]{4,3,2,1,0:T(8,128)(2,1)} %param.11) | copy-start | bytes 1572868
  3.6 7.0 %copy-start.1 = (bf16[1,1,16,16,256]{4,3,2,1,0:T(8,128)(2,1)S(1)}, bf16[1,1,16,16,256]{4,3,2,1,0:T(8,128)(2,1)}, u32[]{:S(2)}) copy-start(bf16[1,1,16,16,256]{4,3,2,1,0:T(8,128)(2,1)} %param.12) | copy-start | bytes 393220
  3.6 12.3 %all-to-all-start = ((bf16[8,3,785]{2,1,0:T(4,128)(2,1)}), bf16[8,3,785]{2,1,0:T(4,128)(2,1)S(1)}, u32[]{:S(2)}, u32[]{:S(2)}) async-start(bf16[8,3,785]{2,1,0:T(4,128)(2,1)} %reshape.74), calls=%async_computation | async-start | bytes 114688 | tf_op jit(solution)/shard_map/all_to_all | solution.py:363
  10.2 0.8 %copy-start.2 = (bf16[80,256]{1,0:T(8,128)(2,1)S(1)}, bf16[80,256]{1,0:T(8,128)(2,1)}, u32[]{:S(2)}) copy-start(bf16[80,256]{1,0:T(8,128)(2,1)} %param.15) | copy-start | bytes 122884
  10.2 1.4 %copy-start.5 = (s32[1,1,24]{2,1,0:T(1,128)S(1)}, s32[1,1,24]{2,1,0:T(1,128)}, u32[]{:S(2)}) copy-start(s32[1,1,24]{2,1,0:T(1,128)} %param.17) | copy-start | bytes 292
  10.2 1.4 %copy-start.6 = (s32[1,1,24]{2,1,0:T(1,128)S(1)}, s32[1,1,24]{2,1,0:T(1,128)}, u32[]{:S(2)}) copy-start(s32[1,1,24]{2,1,0:T(1,128)} %param.16) | copy-start | bytes 292

commit v4 on v3

--- a/solution.py
+++ b/solution.py
@@ -30,11 +30,12 @@
     row_ref,
     col_ref,
     class_ref,
-    tile0_ref,
-    tile1_ref,
+    level_ref,
+    raw0_ref,
+    raw1_ref,
     conv_ref,
     deconv_ref,
-    mask_ref,
+    weight_ref,
     target_ref,
     grad0_ref,
     grad1_ref,
@@ -46,6 +47,9 @@
     pre_scr,
     gmask_ref,
     turned,
+    mask_ref,
+    tile0_ref,
+    tile1_ref,
 ):
     side0, side1, entries, base1 = sizes
     channels = conv_ref.shape[-1]
@@ -53,6 +57,30 @@
     levels = ((tile0_ref, grad0_ref, side0, 1), (tile1_ref, grad1_ref, side1, base1))
 
     halves = channels // 128
+    mask_ref[...] = weight_ref[...].astype(jnp.float32)
+
+    for raw_ref, tile_ref, side in ((raw0_ref, tile0_ref, side0), (raw1_ref, tile1_ref, side1)):
+        for edge in (0, side + 1):
+            tile_ref[:, edge] = jnp.zeros((TAPS, side, channels), jnp.bfloat16)
+        count = 256 // side
+        place = lax.broadcasted_iota(jnp.int32, (256, channels), 0) % side
+
+        def spread(index, carry, raw_ref=raw_ref, tile_ref=tile_ref, side=side, count=count, place=place):
+            start = index * count
+            value = raw_ref[pl.ds(start, count)].astype(jnp.float32) * 0.5
+            value = value.reshape(256, channels)
+            moved = (
+                jnp.where(place == 0, 0.0, pltpu.roll(value, 1, 0)),
+                value,
+                jnp.where(place == side - 1, 0.0, pltpu.roll(value, 255, 0)),
+            )
+            for b in range(TAPS):
+                tile_ref[b, pl.ds(start + 1, count)] = (
+                    moved[b].astype(jnp.bfloat16).reshape(count, side, channels)
+                )
+            return carry
+
+        lax.fori_loop(0, side // count, spread, 0)
 
     def conv_rows(tile_ref, side, base, start, count):
         cells = count * side
@@ -107,7 +135,7 @@
     def some_crops(group, carry):
         crops = [group * GROUP + k for k in range(GROUP)]
         kinds = [class_ref[entry] for entry in crops]
-        rows = [row_ref[entry] for entry in crops]
+        rows = [row_ref[entry] + jnp.where(level_ref[entry] == 0, 1, base1) for entry in crops]
         cols = [col_ref[entry] for entry in crops]
         class_rows = [mask_ref[pl.ds(jnp.maximum(kind, 0), 1), :] for kind in kinds]
         slopes = []
@@ -307,17 +335,6 @@
     out_ref[...] = total
 
 
-def shifted(tile):
-    tile = tile * 0.5
-    return jnp.stack(
-        [
-            jnp.pad(tile, ((1, 1), (1, 0), (0, 0)))[:, :-1],
-            jnp.pad(tile, ((1, 1), (0, 0), (0, 0))),
-            jnp.pad(tile, ((1, 1), (0, 1), (0, 0)))[:, 1:],
-        ]
-    )
-
-
 def on_device(
     level0,
     level1,
@@ -369,10 +386,6 @@
     target = jnp.pad(target, ((0, 0), (0, WIDE - CROP), (0, lanes - entries * 4)))
     target = target.reshape(ROWS, lanes)
 
-    level = crop_level[0, 0]
-    rows = crop_row[0, 0] + jnp.where(level == 0, 1, base1)
-    cols = crop_col[0, 0]
-
     smem = pl.BlockSpec(memory_space=pltpu.SMEM)
     vmem = pl.BlockSpec(memory_space=pltpu.VMEM)
     share = channels // peers
@@ -384,7 +397,7 @@
             jax.ShapeDtypeStruct((side1, side1, channels), jnp.float32),
             jax.ShapeDtypeStruct((peers, height_sent, 128), jnp.float32),
         ),
-        in_specs=[smem] * 3 + [vmem] * 6,
+        in_specs=[smem] * 4 + [vmem] * 6,
         out_specs=(vmem,) * 3,
         scratch_shapes=[
             pltpu.VMEM((3, 3, channels // 128, height, side0 + 8, 128), jnp.float32),
@@ -394,17 +407,21 @@
             pltpu.VMEM((GROUP, ROWS, channels), jnp.float32),
             pltpu.VMEM((128, channels), jnp.float32),
             pltpu.VMEM((channels, 128), jnp.float32),
+            pltpu.VMEM((classes, channels), jnp.float32),
+            pltpu.VMEM((TAPS, side0 + 2, side0, channels), jnp.bfloat16),
+            pltpu.VMEM((TAPS, side1 + 2, side1, channels), jnp.bfloat16),
         ],
         compiler_params=pltpu.CompilerParams(vmem_limit_bytes=60 * 1024 * 1024),
     )(
-        rows,
-        cols,
+        crop_row[0, 0],
+        crop_col[0, 0],
         kinds,
-        shifted(first_tile),
-        shifted(second_tile),
+        crop_level[0, 0],
+        first_tile,
+        second_tile,
         conv_weight,
         deconv_weight.reshape(4, channels, channels),
-        mask_weight.astype(jnp.float32),
+        mask_weight,
         target,
     )
 

time: 60.4 us -> 60.2 us (level)
  waiting for transfers between devices: 1.7 us -> 5.87 us
  other arithmetic: 6.81 us -> 3.38 us
  local copies, waits for them, and re-layouts: 5.29 us -> 4.57 us
    all_to_all x1, waiting for transfers between devices: 1.7 us -> 5.87 us  [on_device(): lax.all_to_all(outgoing, 'tile', split_axis=0, concat_axis=0, tiled=True)]
    another operation x2 -> x0, other arithmetic: 2.17 us -> none  [shifted(): jnp.stack([jnp.pad(tile, ((1, 1), (1, 0), (0, 0)))[:, :-1], jnp.pad(tile,...]
    convert_element_type x1 -> x0, other arithmetic: 0.64 us -> none  [on_device(): mask_weight.astype(jnp.float32)]
  transfers between devices with their start and end apart: 1 -> 1, of which waited for: 1 -> 1; matrix products, arithmetic and copies ran while one was open for 6% -> 0% of each run, Pallas kernels for 0% -> 0%
where the time goes in v4:
time: 60.2 us; the launch traced here: 59.8 us
  Pallas kernels  38.7 us (64%)
  starting transfers between devices  6.33 us (11%)
  waiting for transfers between devices  5.87 us (10%)
  local copies, waits for them, and re-layouts  4.57 us (8%)
  other arithmetic  3.38 us (6%)
  between operations  0.72 us (1%)
    pallas_call x1, Pallas kernels, on_device(): pl.pallas_call(functools.partial(head_kernel, (side0, side1, entries, bas...  26.8 us
    pallas_call x1, Pallas kernels, on_device(): pl.pallas_call(functools.partial(total_kernel, (peers, scenes, share)), o...  11.8 us
    all_to_all x1, starting transfers between devices, on_device(): lax.all_to_all(outgoing, 'tile', split_axis=0, concat_axis=0, tiled=True)  6.33 us
    all_to_all x1, waiting for transfers between devices, on_device(): lax.all_to_all(outgoing, 'tile', split_axis=0, concat_axis=0, tiled=True)  5.87 us
    transpose x1, local copies, waits for them, and re-layouts, on_device(): mask_part = gmask[:, :classes].T  1.32 us
  transfers between devices with their start and end apart: 1, of which 1 were waited for; matrix products, arithmetic and copies ran while one was open for 0% of the time, Pallas kernels for 0%

profile of v4, /device:TPU:0, one launch (start us, length us, event | category | flops | bytes accessed | tf_op | source)
XLA Modules:
  0.0 59.8 jit_solution(3979533530390104829)
XLA Ops:
  0.7 1.2 %convert_element_type.40 = bf16[1,1,22,28,28]{4,1,3,2,0:T(2,128)(2,1)S(1)} convert(s32[1,1,22,28,28]{4,1,3,2,0:T(1,128)} %param.21) | non-fusion elementwise | flops 17248 | bytes 103488 | tf_op jit(solution)/shard_map/convert_element_type | solution.py:368
  1.9 0.3 copy.41
  2.2 0.1 convert_element_type.41
  2.2 0.1 copy.42
  2.4 0.1 copy.43
  2.5 0.1 copy.44
  2.7 0.0 copy-done
  2.7 0.3 convolution_convert_fusion
  2.9 0.7 %reshape.64 = bf16[8,3,785]{2,1,0:T(4,128)(2,1)} reshape(bf16[24,785]{1,0:T(8,128)(2,1)S(1)} %convolution_convert_fusion) | data formatting | bytes 75360 | tf_op jit(solution)/shard_map/reshape | solution.py:379
  3.6 6.3 %all-to-all-start = ((bf16[8,3,785]{2,1,0:T(4,128)(2,1)}), bf16[8,3,785]{2,1,0:T(4,128)(2,1)S(1)}, u32[]{:S(2)}, u32[]{:S(2)}) async-start(bf16[8,3,785]{2,1,0:T(4,128)(2,1)} %reshape.64), calls=%async_computation | async-start | bytes 114688 | tf_op jit(solution)/shard_map/all_to_all | solution.py:380
  9.9 5.9 %all-to-all-done = bf16[8,3,785]{2,1,0:T(4,128)(2,1)S(1)} async-done(((bf16[8,3,785]{2,1,0:T(4,128)(2,1)}), bf16[8,3,785]{2,1,0:T(4,128)(2,1)S(1)}, u32[]{:S(2)}, u32[]{:S(2)}) %all-to-all-start) | async-done | bytes 37712 | tf_op jit(solution)/shard_map/all_to_all | solution.py:380
  15.8 0.7 %add_reduce_fusion.class_ref = s32[24]{0:T(128)} fusion(bf16[24,785]{1,0:T(8,128)(2,1)S(1)} %reshape.65), kind=kLoop, calls=%fused_computation.7 | loop fusion | flops 48 | bytes 144 | tf_op jit(solution)/shard_map/sub | solution.py:383
  16.5 0.2 copy.45
  16.7 0.5 copy.46
  17.2 0.2 copy.47
  17.4 0.7 %bitcast_convert_fusion.target_ref = f32[224,128]{1,0:T(8,128)} fusion(bf16[14,16,128]{2,1,0:T(8,128)(2,1)S(1)} %pad.5), kind=kLoop, calls=%fused_computation.1 | loop fusion | flops 28672 | bytes 172032 | tf_op jit(solution)/shard_map/reshape | solution.py:387
  18.1 26.8 %shard_map.138 = (f32[32,32,256]{2,1,0:T(8,128)}, f32[16,16,256]{2,1,0:T(8,128)}, f32[8,40,128]{2,1,0:T(8,128)}) custom-call(s32[24]{0:T(128)} %bitcast.36, s32[24]{0:T(128)} %bitcast.37, s32[24]{0:T(128)} %add_reduce_fusion.class_ref, s32[24]{0:T(128)} %bitcast.38, bf16[32,32,256]{2,1,0:T(8,128)(2,1)} %bitcast.30, bf16[16,16,256]{2,1,0:T(8,128)(2,1)} %bitcast.33, ...), custom_call_target="tpu_custom_call" | custom-call | tf_op jit(solution)/shard_map/pallas_call | solution.py:393
  44.9 11.8 %shard_map.139 = (f32[32,128]{1,0:T(8,128)}, f32[8,8,128]{2,1,0:T(8,128)}) custom-call(f32[8,40,128]{2,1,0:T(8,128)} %get-tuple-element.11.message_ref), custom_call_target="tpu_custom_call" | custom-call | tf_op jit(solution)/shard_map/pallas_call | solution.py:429
  56.7 0.8 %slice.15 = f32[8,1,128]{2,1,0:T(1,128)S(1)} slice(f32[8,8,128]{2,1,0:T(8,128)} %get-tuple-element.13), slice={[0:8], [0:1], [0:128]} | slice | bytes 8192 | tf_op jit(solution)/shard_map/slice | solution.py:449
  57.5 0.1 dynamic-slice_reduce_fusion
  57.6 0.1 reshape.69
  57.7 0.1 reduce_sum.18
  57.8 0.7 %select_reduce_fusion = f32[22]{0:T(128)} fusion(f32[24]{0:T(128)S(1)} %broadcast_multiply_fusion, s32[22]{0:T(128)S(1)} %bitcast.35), kind=kLoop, calls=%fused_computation.6 | loop fusion | flops 1562 | bytes 272 | tf_op jit(solution)/shard_map/reduce_sum | solution.py:454
  58.5 1.3 %slice_bitcast_fusion = f32[80,32]{0,1:T(8,128)} fusion(f32[32,128]{1,0:T(8,128)} %get-tuple-element.12), kind=kLoop, calls=%fused_computation.5 | loop fusion | bytes 20480 | tf_op jit(solution)/shard_map/transpose | solution.py:448
  (7 shorter events, 0.1 us)
Async XLA Ops:
  0.6 1.9 %copy-start.1 = (s32[1,1,22]{2,1,0:T(1,128)S(1)}, s32[1,1,22]{2,1,0:T(1,128)}, u32[]{:S(2)}) copy-start(s32[1,1,22]{2,1,0:T(1,128)} %param.20) | copy-start | bytes 268
  0.6 2.0 %copy-start = (s32[1,1,22]{2,1,0:T(1,128)S(1)}, s32[1,1,22]{2,1,0:T(1,128)}, u32[]{:S(2)}) copy-start(s32[1,1,22]{2,1,0:T(1,128)} %param.19) | copy-start | bytes 268
  3.6 12.2 %all-to-all-start = ((bf16[8,3,785]{2,1,0:T(4,128)(2,1)}), bf16[8,3,785]{2,1,0:T(4,128)(2,1)S(1)}, u32[]{:S(2)}, u32[]{:S(2)}) async-start(bf16[8,3,785]{2,1,0:T(4,128)(2,1)} %reshape.64), calls=%async_computation | async-start | bytes 114688 | tf_op jit(solution)/shard_map/all_to_all | solution.py:380
